TPU v7x, 32 devices: a whole 2x2x4 slice. The times are simulated.
32 devices in a mesh: ctx: 4 (over y, core), enc: 8 (over z, x).
Axes of the slice: x: 2, y: 2, z: 4, core: 2. Of those that a mesh axis runs over, the one named last changes fastest.
Arguments:
- queries: bfloat16 [8, 512, 4096], P('enc', 'ctx'), may hold values from -200 to 200
- d_out: bfloat16 [8, 512, 4096], P('enc', 'ctx'), may hold values from -24 to 24
- text_sample: int32 [8, 512], P('enc', 'ctx'), may hold values from 0 to 1, as said below
- tiles: int32 [8, 2], P('enc'), may hold values from 1 to 4
- img_k: bfloat16 [8, 512, 1024], P(None, ('ctx', 'enc')), may hold values from -20 to 20
- img_v: bfloat16 [8, 512, 1024], P(None, ('ctx', 'enc')), may hold values from -6 to 6
Outputs:
- d_queries: bfloat16 [8, 512, 4096], P('enc', 'ctx')
- d_img_k: bfloat16 [8, 512, 1024], P(None, ('ctx', 'enc'))
- d_img_v: bfloat16 [8, 512, 1024], P(None, ('ctx', 'enc'))
Inputs may be any that keep to these rules, and one draw needn't show every extreme that they name: `text_sample`: within each group the sample numbers never fall along the text, and each of the 2 samples has at least one token.
All inputs are finite; a program needn't handle non-finite values.
Results may differ from a plain program's by a relative error of at most 0.022.
Values may be sent and summed in bfloat16 or wider, within the bound.
No kernel may reach another device: no remote copies, remote signals or barrier semaphores. Data moves between devices by JAX's collectives and lax.ppermute only.
A program may use at most 128 MiB of HBM per device.

v0:
```python
import functools

import jax
import jax.numpy as jnp
from jax import lax
from jax.experimental import pallas as pl
from jax.experimental.pallas import tpu as pltpu
from jax.sharding import PartitionSpec as P

H = 32
KVH = 8
HD = 128
SAMP = 2
MAX_TILES = 4
TILE_TOK = 64
RATIO = H // KVH
CORES = 2
SLOT_ROWS = MAX_TILES * TILE_TOK
HALF_KV = KVH // CORES
HALF_KCOLS = HALF_KV * HD
HALF_QCOLS = HALF_KCOLS * RATIO
WIDE = RATIO * HD
SAMP_ROWS = 16
SCALE = HD ** (-0.5)
LOG2E = 1.4426950408889634
BIG_NEGATIVE = -1e30
NT = (((1,), (1,)), ((), ()))
TN = (((0,), (0,)), ((), ()))
BF16 = jnp.bfloat16
F32 = jnp.float32

IN_VMEM = pl.BlockSpec(memory_space=pltpu.VMEM)
IN_HBM = pl.BlockSpec(memory_space=pltpu.HBM)


def local_call(body, ins, outs, scratch=(), flops=0, moved=2**19, aliases={}):
    return pl.pallas_call(
        body,
        in_specs=ins,
        out_specs=[spec for _, _, spec in outs],
        out_shape=[jax.ShapeDtypeStruct(s, d) for s, d, _ in outs],
        scratch_shapes=list(scratch),
        compiler_params=pltpu.CompilerParams(vmem_limit_bytes=8 * 2**20),
        input_output_aliases=aliases,
        cost_estimate=pl.CostEstimate(
            flops=flops, bytes_accessed=moved, transcendentals=flops // 1280
        ),
    )


def in_vmem(body, outs, **more):
    def call(*args):
        spec = [(shape, dtype, IN_VMEM) for shape, dtype in outs]
        return local_call(body, [IN_VMEM] * len(args), spec, **more)(*args)

    return call


def core_of():
    return lax.rem(lax.axis_index("ctx"), CORES)


def at_rows(first, count):
    return pl.ds(pl.multiple_of(first, count), count)


def at_cols(first, width, step):
    return pl.ds(pl.multiple_of(first, step), width)


def start_copies(pairs, sems):
    copies = [pltpu.make_async_copy(src, dst, sems.at[i]) for i, (src, dst) in enumerate(pairs)]
    for copy in copies:
        copy.start()
    return copies


def run_copies(pairs, sems):
    for copy in start_copies(pairs, sems):
        copy.wait()


def in_hbm(*arrays):
    return [pltpu.with_memory_space_constraint(a, pltpu.HBM) for a in arrays]


def split_kernel(k_ref, v_ref, mine, peer, sems):
    core = core_of()
    pairs = []
    for half, out in ((1 - core, peer), (core, mine)):
        cols = at_cols(half * HALF_KCOLS, HALF_KCOLS, HALF_KCOLS)
        for i, ref in enumerate((k_ref, v_ref)):
            pairs.append((ref.at[:, :, cols], out.at[i]))
    run_copies(pairs, sems)


def near_place():
    return lax.div(lax.axis_index("ctx"), CORES), lax.axis_index("enc")


def split_text(n_blocks, pieces, where, q_ref, g_ref, samp_hbm, tiles_hbm, peer, q_own, g_own, bias, samp, tiles, sems):
    core = core_of()
    tokens = q_ref.shape[1]
    own_cols = at_cols(core * HALF_QCOLS, HALF_QCOLS, HALF_QCOLS)
    peer_cols = at_cols((1 - core) * HALF_QCOLS, HALF_QCOLS, HALF_QCOLS)
    copies = start_copies(
        [
            (samp_hbm, samp),
            (tiles_hbm, tiles),
            (q_ref.at[0, :, peer_cols], peer.at[:tokens]),
            (g_ref.at[0, :, peer_cols], peer.at[tokens : 2 * tokens]),
            (q_ref.at[0, :, own_cols], q_own.at[:tokens]),
            (g_ref.at[0, :, own_cols], g_own),
        ],
        sems,
    )
    for copy in copies[:2]:
        copy.wait()
    row = jnp.broadcast_to(samp[...].astype(F32), (SAMP_ROWS, tokens)).astype(BF16)
    for out, first in ((q_own, tokens), (peer, 2 * tokens)):
        out[first:, :] = jnp.zeros((SAMP_ROWS, HALF_QCOLS), BF16)
        out[first:, :tokens] = row

    sample, enc = where()
    block_rows = SLOT_ROWS // n_blocks
    slots = block_rows // pieces
    line = lax.broadcasted_iota(jnp.int32, (SLOT_ROWS, HD), 0)
    block = lax.div(line, block_rows)
    if n_blocks > 1:
        low, high = block & 1, lax.div(block, 2) & 1
        block = block - low - 2 * high + 2 * low + high
    owner = block ^ enc
    piece = lax.rem(lax.div(line, slots), pieces)
    slot = piece * (SLOT_ROWS // pieces) + owner * slots + lax.rem(line, slots)
    for i in range(SAMP):
        count = jnp.where((sample ^ i) == 0, tiles[0:1, 0:1], tiles[0:1, 1:2])
        bias[i] = jnp.where(slot < count * TILE_TOK, 0.0, BIG_NEGATIVE)
    for copy in copies[2:]:
        copy.wait()


def carry_kernel(slots, own, got, text, *outs):
    core = core_of()
    enc = lax.axis_index("enc")
    for dz, out in enumerate(outs[:-1]):
        for dx in range(2):
            group = enc ^ (2 * dz + dx)
            for i in range(2):
                first = i * CORES * slots
                out[dx, at_rows(first + core * slots, slots), :] = own[i, group]
                out[dx, at_rows(first + (1 - core) * slots, slots), :] = got[i, group]


def join_kernel(*refs):
    parts, outs = refs[:2], refs[-2:]
    rows = parts[0].shape[1]
    for dx, out in enumerate(outs):
        for dz, part in enumerate(parts):
            out[dz * rows : (dz + 1) * rows, :] = part[dx]


def block_place(b, n_outs):
    half, x, z = b // 4, b // 2 % 2, b % 2
    return {1: (0, b), 2: (x, 2 * half + z), 4: (2 * half + x, z)}[n_outs]


def add_kernel(z, own, back_x, back_y, back_xy, *outs):
    rows = outs[0].shape[1]
    for dz, out in enumerate(outs):
        near = slice((z + dz) * rows, (z + dz + 1) * rows)
        far = slice(dz * rows, (dz + 1) * rows)
        for dx, (here, back) in enumerate(((own, back_y), (back_x, back_xy))):
            out[dx] = (here[near, :].astype(F32) + back[far, :].astype(F32)).astype(out.dtype)


def nothing_kernel(*refs):
    pass


def hand_on(array, *after):
    return in_vmem(nothing_kernel, [(array.shape, array.dtype)], aliases={0: 0})(array, *after)


def far_rows_kernel(slots, *refs):
    core = core_of()
    parts, outs = refs[:2], refs[-2:]
    for dz, part in enumerate(parts):
        for dx in range(2):
            for i in range(2):
                first = i * CORES * slots
                for who, out in zip((core, 1 - core), outs):
                    out[i, 2 * dz + dx] = part[dx, at_rows(first + who * slots, slots), :]


def owner_rows_kernel(slots, *refs):
    core = core_of()
    enc = lax.axis_index("enc")
    parts, far, outs = refs[:2], refs[2:4], refs[4:]
    for dz, part in enumerate(parts):
        for dx in range(2):
            d = 2 * dz + dx
            for i in range(2):
                first = i * CORES * slots
                for who, from_far, out in zip((core, 1 - core), far, outs):
                    out[i, enc ^ d] = part[dx, at_rows(first + who * slots, slots), :]
                    out[i, enc ^ (2 * len(parts) + d)] = from_far[i, d]


def finish_kernel(mine, got, dk, dv, sems):
    core = core_of()
    pairs = []
    for half, ref in ((core, mine), (1 - core, got)):
        cols = at_cols(half * HALF_KCOLS, HALF_KCOLS, HALF_KCOLS)
        for i, out in enumerate((dk, dv)):
            pairs.append((ref.at[i], out.at[:, :, cols]))
    run_copies(pairs, sems)


def finish_text_kernel(mine, got, out, sems):
    core = core_of()
    pairs = []
    for half, ref in ((core, mine), (1 - core, got)):
        pairs.append((ref, out.at[0, :, at_cols(half * HALF_QCOLS, HALF_QCOLS, HALF_QCOLS)]))
    run_copies(pairs, sems)


def pass_kernel(role, n_blocks, n_kv, with_prev, n_through, n_grads, where, bias, q_a, g_a, got, *rest):
    kvs, rest = rest[:n_kv], rest[n_kv:]
    prev = None
    if with_prev:
        prev, rest = rest[:2], rest[2:]
    rest = rest[n_through:]
    dqs, grads = rest[:2], rest[2 : 2 + n_grads]
    sample = where()[0] ^ role
    tokens = g_a.shape[0]
    block_rows = SLOT_ROWS // n_blocks
    row_a = q_a[tokens : tokens + 1, :tokens].astype(F32)
    row_b = got[2 * tokens : 2 * tokens + 1, :tokens].astype(F32)
    wanted = sample.astype(F32)
    has = jnp.where(row_a == wanted, 1.0, jnp.where(row_b == wanted, 1.0, 0.0))
    present = jnp.max(has) > 0.5

    @pl.when(present)
    def _():
        mine = jnp.concatenate([row_a] * RATIO + [row_b] * RATIO, axis=1) == wanted
        for h in range(HALF_KV):
            first_q = h * WIDE
            first_k = h * HD

            def stacked(ref_a, first_b):
                parts = [
                    ref[first : first + tokens, first_q + r * HD : first_q + (r + 1) * HD]
                    for ref, first in ((ref_a, 0), (got, first_b))
                    for r in range(RATIO)
                ]
                return jnp.concatenate(parts, axis=0)

            def rows_of(first):
                parts = []
                for kv in kvs:
                    for at in range(first, kv.shape[0], 2 * block_rows):
                        parts.append(kv[at : at + block_rows, first_k : first_k + HD])
                return jnp.concatenate(parts, axis=0)

            q = stacked(q_a, 0)
            g = stacked(g_a, tokens)
            k = rows_of(0)
            v = rows_of(block_rows)
            s = lax.dot_general(k, q, NT, preferred_element_type=F32)
            s = s + jnp.concatenate([bias[role]] * (s.shape[1] // HD), axis=1)
            top = jnp.max(s, axis=0, keepdims=True)
            e = jnp.exp2((s - top) * (SCALE * LOG2E))
            total = jnp.sum(e, axis=0, keepdims=True)
            p = e * jnp.where(mine, 1.0 / total, 0.0)
            gp = lax.dot_general(v, g, NT, preferred_element_type=F32)
            row_dot = jnp.sum(p * gp, axis=0, keepdims=True)
            ds = (p * (gp - row_dot)).astype(BF16)
            dv = jnp.dot(p.astype(BF16), g, preferred_element_type=F32)
            dk = jnp.dot(ds, q, preferred_element_type=F32) * SCALE
            dq = lax.dot_general(ds, k, TN, preferred_element_type=F32) * SCALE
            for t, dq_ref in enumerate(dqs):
                for r in range(RATIO):
                    at = (t * RATIO + r) * tokens
                    cols = slice(first_q + r * HD, first_q + (r + 1) * HD)
                    part = dq[at : at + tokens]
                    if with_prev:
                        part = part + prev[t][:, cols].astype(F32)
                    dq_ref[:, cols] = part.astype(dq_ref.dtype)
            cols = slice(first_k, first_k + HD)
            for b in range(n_blocks):
                rows = slice(b * block_rows, (b + 1) * block_rows)
                dx, at = block_place(b, len(grads))
                out, first = grads[dx], at * 2 * block_rows
                out[first : first + block_rows, cols] = dk[rows].astype(out.dtype)
                out[first + block_rows : first + 2 * block_rows, cols] = dv[rows].astype(out.dtype)

    @pl.when(jnp.logical_not(present))
    def _():
        for out in grads:
            out[...] = jnp.zeros_like(out)
        for t, dq_ref in enumerate(dqs):
            dq_ref[...] = prev[t][...] if with_prev else jnp.zeros_like(dq_ref)


def sample_pass(where, role, n_blocks, bias, text, kvs, prev, grads, through=()):
    tokens = text[1].shape[0]
    dq = ((tokens, HALF_QCOLS), BF16)
    args = [bias, *text, *kvs, *(prev or ())]
    dq_a, dq_b, *outs = in_vmem(
        functools.partial(
            pass_kernel, role, n_blocks, len(kvs), prev is not None, len(through), len(grads), where
        ),
        [dq, dq, *grads] + [(a.shape, a.dtype) for a in through],
        flops=10 * tokens * WIDE * SLOT_ROWS * CORES * HALF_KV,
        moved=16 * 2**20,
        aliases={len(args) + i: 2 + len(grads) + i for i in range(len(through))},
    )(*args, *through)
    return (dq_a, dq_b), outs


def shards(n_ctx, n_enc, queries, d_out, text_sample, tiles, img_k, img_v):
    n_y = n_ctx // CORES
    slots = img_k.shape[1]
    tokens = queries.shape[1]
    swap_core = [(i, i ^ 1) for i in range(n_ctx)]
    near = n_y == SAMP and slots % 16 == 0 and n_enc == 8
    text_outs = [
        ((2 * tokens + SAMP_ROWS, HALF_QCOLS), BF16, IN_VMEM),
        ((tokens + SAMP_ROWS, HALF_QCOLS), BF16, IN_VMEM),
        ((tokens, HALF_QCOLS), BF16, IN_VMEM),
        ((SAMP, SLOT_ROWS, HD), F32, IN_VMEM),
    ]

    def split_the_text(n_blocks, pieces, where):
        return local_call(
            functools.partial(split_text, n_blocks, pieces, where),
            [IN_HBM] * 4,
            text_outs,
            [
                pltpu.VMEM(text_sample.shape, jnp.int32),
                pltpu.VMEM(tiles.shape, jnp.int32),
                pltpu.SemaphoreType.DMA((6,)),
            ],
            moved=4 * 2**20,
        )(*in_hbm(queries, d_out, text_sample, tiles))

    if near:
        swap_y = [(i, (i + CORES) % n_ctx) for i in range(n_ctx)]
        n_z = n_enc // 2
        block_rows = 2 * CORES * slots
        pair = (2, block_rows, HALF_KCOLS)
        quarter = (2 * block_rows, HALF_KCOLS)
        whole = (SLOT_ROWS, HALF_KCOLS)
        kv_halves = (2, n_enc, slots, HALF_KCOLS)
        swap_x = [(i, i ^ 1) for i in range(n_enc)]
        swap_xy = [
            (i * n_enc + e, (i + CORES) % n_ctx * n_enc + (e ^ 1))
            for i in range(n_ctx)
            for e in range(n_enc)
        ]

        def along_z(part, dz):
            return lax.ppermute(part, "enc", [(i, i ^ (2 * dz)) for i in range(n_enc)]) if dz else part

        def along_x(part):
            return lax.ppermute(part, "enc", swap_x)

        def along_y(part):
            return lax.ppermute(part, "ctx", swap_y)

        def along_xy(part):
            return lax.ppermute(part, ("ctx", "enc"), swap_xy)

        mine, for_peer = local_call(
            split_kernel,
            [IN_HBM] * 2,
            [(kv_halves, BF16, IN_VMEM)] * 2,
            [pltpu.SemaphoreType.DMA((4,))],
        )(*in_hbm(img_k, img_v))
        text_peer, q_own, g_own, bias = split_the_text(n_enc, CORES, near_place)
        *carry, text_peer = in_vmem(
            functools.partial(carry_kernel, slots),
            [(pair, BF16)] * n_z + [(text_peer.shape, BF16)],
            aliases={2: n_z},
        )(mine, lax.ppermute(for_peer, "ctx", swap_core), text_peer)
        text = (q_own, g_own, lax.ppermute(text_peer, "ctx", swap_core))

        came = [along_z(part, dz) for dz, part in enumerate(carry)]
        own, far = [], []
        for z in (0, 2):
            here, beside = in_vmem(join_kernel, [(quarter, BF16)] * 2)(
                *came[z : z + 2], text[2], *far
            )
            own += [here, along_x(beside)]
            far += [along_y(here), along_xy(beside)]
        own_dq, (own_here, own_beside) = sample_pass(
            near_place, 0, n_enc, bias, text, own, None, [(whole, F32), (whole, BF16)]
        )
        (own_beside,) = hand_on(own_beside, far[2])
        back_x = along_x(own_beside)
        dq, far_grads = sample_pass(
            near_place, 1, n_enc, bias, text, far, own_dq, [(quarter, BF16)] * 4
        )
        dq_got = lax.ppermute(dq[1], "ctx", swap_core)
        returned = [None] * n_z
        for z in (2, 0):
            here, beside = far_grads[z : z + 2]
            totals = in_vmem(functools.partial(add_kernel, z), [(pair, BF16)] * 2)(
                own_here, back_x, along_y(here), along_xy(beside)
            )
            for dz, total in enumerate(totals, z):
                returned[dz] = along_z(total, dz)
    else:
        both = ("ctx", "enc")
        same_y = [
            [yy * CORES * n_enc + i for i in range(CORES * n_enc)] for yy in range(n_y)
        ]
        same_column = [
            [(yy * CORES + c) * n_enc + e for yy in range(n_y)]
            for c in range(CORES)
            for e in range(n_enc)
        ]
        core = core_of()

        def exchange(parts):
            return lax.all_to_all(
                parts, both, split_axis=0, concat_axis=0, axis_index_groups=same_y, tiled=True
            )

        def to_groups(owned):
            parts = owned.reshape(n_enc, slots, CORES, HALF_KCOLS).transpose(2, 0, 1, 3)
            got = exchange(parts.reshape(CORES * n_enc, slots, HALF_KCOLS))
            got = got.reshape(CORES * n_enc * slots, HALF_KCOLS)
            return lax.all_gather(got, both, axis=0, axis_index_groups=same_column, tiled=True)

        def to_owners(grads):
            grads = lax.psum_scatter(
                grads, both, scatter_dimension=0, axis_index_groups=same_column, tiled=True
            )
            got = exchange(grads.reshape(CORES * n_enc, slots, HALF_KCOLS))
            got = got.reshape(CORES, n_enc, slots, HALF_KCOLS).transpose(1, 2, 0, 3)
            return got.reshape(n_enc, slots, CORES * HALF_KCOLS)

        def no_place():
            return jnp.int32(0), jnp.int32(0)

        all_k = to_groups(img_k)
        all_v = to_groups(img_v)
        text_peer, q_own, g_own, bias = split_the_text(1, 1, no_place)
        text = (q_own, g_own, lax.ppermute(text_peer, "ctx", swap_core))
        kvs = [
            jnp.concatenate([part[s * SLOT_ROWS : (s + 1) * SLOT_ROWS] for part in (all_k, all_v)], axis=0)
            for s in range(SAMP)
        ]
        dq, grads = None, []
        for sample, kv in enumerate(kvs):
            dq, grad = sample_pass(no_place, sample, 1, bias, text, [kv], dq, [(kv.shape, BF16)])
            grads += grad
        d_img_k = to_owners(jnp.concatenate([g[:SLOT_ROWS] for g in grads], axis=0))
        d_img_v = to_owners(jnp.concatenate([g[SLOT_ROWS:] for g in grads], axis=0))
        dq_got = lax.ppermute(dq[1], "ctx", swap_core)

    (d_queries,) = local_call(
        finish_text_kernel,
        [IN_VMEM] * 2,
        [(queries.shape, BF16, IN_HBM)],
        [pltpu.SemaphoreType.DMA((2,))],
    )(dq[0], dq_got)
    if near:
        far_rows = in_vmem(
            functools.partial(far_rows_kernel, slots),
            [((2, n_enc // 2, slots, HALF_KCOLS), BF16)] * 2,
        )(*returned[2:])
        mine, for_peer = in_vmem(
            functools.partial(owner_rows_kernel, slots), [(kv_halves, BF16)] * 2
        )(*returned[:2], *far_rows)
        d_img_k, d_img_v = local_call(
            finish_kernel,
            [IN_VMEM] * 2,
            [(img_k.shape, BF16, IN_HBM)] * 2,
            [pltpu.SemaphoreType.DMA((4,))],
        )(mine, lax.ppermute(for_peer, "ctx", swap_core))
    return (d_queries, d_img_k, d_img_v)


def solution(mesh):
    in_specs = (
        P("enc", "ctx", None),
        P("enc", "ctx", None),
        P("enc", "ctx"),
        P("enc", None),
        P(None, ("ctx", "enc"), None),
        P(None, ("ctx", "enc"), None),
    )
    out_specs = (
        P("enc", "ctx", None),
        P(None, ("ctx", "enc"), None),
        P(None, ("ctx", "enc"), None),
    )
    body = functools.partial(shards, mesh.shape["ctx"], mesh.shape["enc"])
    return jax.shard_map(body, mesh=mesh, in_specs=in_specs, out_specs=out_specs, check_vma=False)
```

profile of v0, /device:TPU:0, one launch (start us, length us, event | category | flops | bytes accessed | tf_op | source)
XLA Modules:
  0.0 62.5 jit_solution(12464571341358775432)
XLA Ops:
  0.6 1.1 %shard_map.86 = (bf16[2,8,16,512]{3,2,1,0:T(8,128)(2,1)S(1)}, bf16[2,8,16,512]{3,2,1,0:T(8,128)(2,1)S(1)}) custom-call(bf16[8,16,1024]{2,1,0:T(8,128)(2,1)} %k_ref.1, bf16[8,16,1024]{2,1,0:T(8,128)(2,1)} %v_ref.1), custom_call_target="tpu_custom_call" | custom-call | bytes 524288 | tf_op jit(solution)/shard_map/pallas_call | solution.py:374
  1.8 0.5 collective-permute-start
  2.3 1.6 %shard_map.85 = (bf16[272,2048]{1,0:T(8,128)(2,1)S(1)}, bf16[144,2048]{1,0:T(8,128)(2,1)S(1)}, bf16[128,2048]{1,0:T(8,128)(2,1)S(1)}, f32[2,256,128]{2,1,0:T(8,128)S(1)}) custom-call(bf16[1,128,4096]{2,1,0:T(8,128)(2,1)} %q_ref.1, bf16[1,128,4096]{2,1,0:T(8,128)(2,1)} %g_ref.1, s32[1,128]{1,0:T(1,128)} %samp_hbm.1, s32[1,2]{1,0:T(1,128)} %tiles_hbm.1), custom_call_target="tpu_custom_call" | custom-call | bytes 4194304 | tf_op jit(solution)/shard_map/pallas_call | solution.py:335
  3.9 0.0 collective-permute-done.got
  3.9 0.1 shard_map.87
  4.0 0.1 collective-permute-start.1
  4.1 3.0 %collective-permute-start.2 = (bf16[2,64,512]{2,1,0:T(8,128)(2,1)S(1)}, bf16[2,64,512]{2,1,0:T(8,128)(2,1)S(1)}, u32[]{:S(2)}, u32[]{:S(2)}) collective-permute-start(bf16[2,64,512]{2,1,0:T(8,128)(2,1)S(1)} %get-tuple-element.46), channel_id=1, source_target_pairs={{0,2},{1,3},{2,0},{3,1},{4,6},{5,7},{6,4},{7,5},{8,10},{9,11},{10,... | collective-permute-start | bytes 393224 | tf_op jit(solution)/shard_map/ppermute | solution.py:363
  7.1 2.6 %collective-permute-start.5 = (bf16[2,64,512]{2,1,0:T(8,128)(2,1)S(1)}, bf16[2,64,512]{2,1,0:T(8,128)(2,1)S(1)}, u32[]{:S(2)}, u32[]{:S(2)}) collective-permute-start(bf16[2,64,512]{2,1,0:T(8,128)(2,1)S(1)} %get-tuple-element.49), channel_id=1, source_target_pairs={{0,4},{1,5},{2,6},{3,7},{4,0},{5,1},{6,2},{7,3},{8,12},{9,13},{10,... | collective-permute-start | bytes 393224 | tf_op jit(solution)/shard_map/ppermute | solution.py:363
  9.7 0.0 collective-permute-start.6
  9.7 3.0 %collective-permute-done.2.refs_1_ = bf16[2,64,512]{2,1,0:T(8,128)(2,1)S(1)} collective-permute-done((bf16[2,64,512]{2,1,0:T(8,128)(2,1)S(1)}, bf16[2,64,512]{2,1,0:T(8,128)(2,1)S(1)}, u32[]{:S(2)}, u32[]{:S(2)}) %collective-permute-start.2) | collective-permute-done | bytes 131104 | tf_op jit(solution)/shard_map/ppermute | solution.py:363
  12.7 0.0 collective-permute-done.1.refs_2_.got
  12.7 1.8 %collective-permute-start.3 = (bf16[128,512]{1,0:T(8,128)(2,1)S(1)}, bf16[128,512]{1,0:T(8,128)(2,1)S(1)}, u32[]{:S(2)}, u32[]{:S(2)}) collective-permute-start(bf16[128,512]{1,0:T(8,128)(2,1)S(1)} %get-tuple-element.47.rest_0_), channel_id=1, source_target_pairs={{0,16},{8,24},{16,0},{24,8},{1,17},{9,25},{17,1},{25,9},{2,18},{10... | collective-permute-start | bytes 393224 | tf_op jit(solution)/shard_map/ppermute | solution.py:369
  14.5 1.4 %collective-permute-start.4 = (bf16[128,512]{1,0:T(8,128)(2,1)S(1)}, bf16[128,512]{1,0:T(8,128)(2,1)S(1)}, u32[]{:S(2)}, u32[]{:S(2)}) collective-permute-start(bf16[128,512]{1,0:T(8,128)(2,1)S(1)} %get-tuple-element.48), channel_id=1, source_target_pairs={{0,17},{1,16},{2,19},{3,18},{4,21},{5,20},{6,23},{7,22},{8,25},{9,... | collective-permute-start | bytes 393224 | tf_op jit(solution)/shard_map/ppermute | solution.py:372
  15.9 0.3 collective-permute-start.9
  16.3 3.8 %collective-permute-done.5.refs_0_ = bf16[2,64,512]{2,1,0:T(8,128)(2,1)S(1)} collective-permute-done((bf16[2,64,512]{2,1,0:T(8,128)(2,1)S(1)}, bf16[2,64,512]{2,1,0:T(8,128)(2,1)S(1)}, u32[]{:S(2)}, u32[]{:S(2)}) %collective-permute-start.5) | collective-permute-done | bytes 131104 | tf_op jit(solution)/shard_map/ppermute | solution.py:363
  20.0 0.0 collective-permute-done.6.refs_1_
  20.0 0.0 collective-permute-done.3.refs_3_.rest_0_
  20.0 0.3 collective-permute-done.4.refs_4_.rest_1_
  20.4 1.6 %collective-permute-start.10 = (bf16[128,512]{1,0:T(8,128)(2,1)S(1)}, bf16[128,512]{1,0:T(8,128)(2,1)S(1)}, u32[]{:S(2)}, u32[]{:S(2)}) collective-permute-start(bf16[128,512]{1,0:T(8,128)(2,1)S(1)} %get-tuple-element.52), channel_id=1, source_target_pairs={{0,1},{1,0},{2,3},{3,2},{4,5},{5,4},{6,7},{7,6},{8,9},{9,8},{10,11... | collective-permute-start | bytes 393224 | tf_op jit(solution)/shard_map/ppermute | solution.py:366
  22.0 1.2 %collective-permute-start.7 = (bf16[128,512]{1,0:T(8,128)(2,1)S(1)}, bf16[128,512]{1,0:T(8,128)(2,1)S(1)}, u32[]{:S(2)}, u32[]{:S(2)}) collective-permute-start(bf16[128,512]{1,0:T(8,128)(2,1)S(1)} %get-tuple-element.51.rest_2_), channel_id=1, source_target_pairs={{0,16},{8,24},{16,0},{24,8},{1,17},{9,25},{17,1},{25,9},{2,18},{10... | collective-permute-start | bytes 393224 | tf_op jit(solution)/shard_map/ppermute | solution.py:369
  23.1 0.8 %collective-permute-start.8 = (bf16[128,512]{1,0:T(8,128)(2,1)S(1)}, bf16[128,512]{1,0:T(8,128)(2,1)S(1)}, u32[]{:S(2)}, u32[]{:S(2)}) collective-permute-start(bf16[128,512]{1,0:T(8,128)(2,1)S(1)} %get-tuple-element.52), channel_id=1, source_target_pairs={{0,17},{1,16},{2,19},{3,18},{4,21},{5,20},{6,23},{7,22},{8,25},{9,... | collective-permute-start | bytes 393224 | tf_op jit(solution)/shard_map/ppermute | solution.py:372
  24.0 0.0 collective-permute-done.9.rest_1_
  24.0 1.9 %collective-permute-done.10.rest_3_ = bf16[128,512]{1,0:T(8,128)(2,1)S(1)} collective-permute-done((bf16[128,512]{1,0:T(8,128)(2,1)S(1)}, bf16[128,512]{1,0:T(8,128)(2,1)S(1)}, u32[]{:S(2)}, u32[]{:S(2)}) %collective-permute-start.10) | collective-permute-done | bytes 131104 | tf_op jit(solution)/shard_map/ppermute | solution.py:366
  25.9 4.3 %shard_map.90 = (bf16[128,2048]{1,0:T(8,128)(2,1)S(1)}, bf16[128,2048]{1,0:T(8,128)(2,1)S(1)}, f32[256,512]{1,0:T(8,128)S(1)}, bf16[256,512]{1,0:T(8,128)(2,1)S(1)}) custom-call(f32[2,256,128]{2,1,0:T(8,128)S(1)} %get-tuple-element.38.bias, bf16[144,2048]{1,0:T(8,128)(2,1)S(1)} %get-tuple-element.39.q_a, bf16[128,2048]{1,0:T(8,128)(2,1)S(1)} %get-tuple-element.40.g_a, ...), custom_call_target="tpu_custom_call" | custom-call | flops 1342177280 | bytes 16777216 | tf_op jit(solution)/shard_map/pallas_call | solution.py:54
  30.2 0.0 collective-permute-done.7.rest_2_.refs_1_
  30.2 1.1 %collective-permute-start.12 = (bf16[256,512]{1,0:T(8,128)(2,1)S(1)}, bf16[256,512]{1,0:T(8,128)(2,1)S(1)}, u32[]{:S(2)}, u32[]{:S(2)}) collective-permute-start(bf16[256,512]{1,0:T(8,128)(2,1)S(1)} %shard_map.93), channel_id=1, source_target_pairs={{0,1},{1,0},{2,3},{3,2},{4,5},{5,4},{6,7},{7,6},{8,9},{9,8},{10,11... | collective-permute-start | bytes 786440 | tf_op jit(solution)/shard_map/ppermute | solution.py:366
  31.3 0.0 collective-permute-done.8.rest_3_
  31.3 0.2 shard_map.91
  31.5 5.4 %collective-permute-start.16 = (bf16[128,512]{1,0:T(8,128)(2,1)S(1)}, bf16[128,512]{1,0:T(8,128)(2,1)S(1)}, u32[]{:S(2)}, u32[]{:S(2)}) collective-permute-start(bf16[128,512]{1,0:T(8,128)(2,1)S(1)} %get-tuple-element.63), channel_id=1, source_target_pairs={{0,16},{8,24},{16,0},{24,8},{1,17},{9,25},{17,1},{25,9},{2,18},{10... | collective-permute-start | bytes 393224 | tf_op jit(solution)/shard_map/ppermute | solution.py:369
  36.9 0.8 %collective-permute-start.17 = (bf16[128,512]{1,0:T(8,128)(2,1)S(1)}, bf16[128,512]{1,0:T(8,128)(2,1)S(1)}, u32[]{:S(2)}, u32[]{:S(2)}) collective-permute-start(bf16[128,512]{1,0:T(8,128)(2,1)S(1)} %get-tuple-element.64), channel_id=1, source_target_pairs={{0,17},{1,16},{2,19},{3,18},{4,21},{5,20},{6,23},{7,22},{8,25},{9,... | collective-permute-start | bytes 393224 | tf_op jit(solution)/shard_map/ppermute | solution.py:372
  37.7 1.9 %collective-permute-start.13 = (bf16[128,512]{1,0:T(8,128)(2,1)S(1)}, bf16[128,512]{1,0:T(8,128)(2,1)S(1)}, u32[]{:S(2)}, u32[]{:S(2)}) collective-permute-start(bf16[128,512]{1,0:T(8,128)(2,1)S(1)} %get-tuple-element.59), channel_id=1, source_target_pairs={{0,16},{8,24},{16,0},{24,8},{1,17},{9,25},{17,1},{25,9},{2,18},{10... | collective-permute-start | bytes 393224 | tf_op jit(solution)/shard_map/ppermute | solution.py:369
  39.6 0.3 collective-permute-start.14
  39.9 3.6 %collective-permute-done.16.back_y = bf16[128,512]{1,0:T(8,128)(2,1)S(1)} collective-permute-done((bf16[128,512]{1,0:T(8,128)(2,1)S(1)}, bf16[128,512]{1,0:T(8,128)(2,1)S(1)}, u32[]{:S(2)}, u32[]{:S(2)}) %collective-permute-start.16) | collective-permute-done | bytes 131104 | tf_op jit(solution)/shard_map/ppermute | solution.py:369
  43.5 0.0 collective-permute-start.11
  43.5 0.0 collective-permute-done.17.back_xy
  43.5 0.0 collective-permute-done.12.back_x
  43.5 0.1 shard_map.95
  43.6 5.2 %collective-permute-start.18 = (bf16[2,64,512]{2,1,0:T(8,128)(2,1)S(1)}, bf16[2,64,512]{2,1,0:T(8,128)(2,1)S(1)}, u32[]{:S(2)}, u32[]{:S(2)}) collective-permute-start(bf16[2,64,512]{2,1,0:T(8,128)(2,1)S(1)} %get-tuple-element.65), channel_id=1, source_target_pairs={{0,4},{1,5},{2,6},{3,7},{4,0},{5,1},{6,2},{7,3},{8,12},{9,13},{10,... | collective-permute-start | bytes 393224 | tf_op jit(solution)/shard_map/ppermute | solution.py:363
  48.8 0.3 collective-permute-start.19
  49.1 0.1 shard_map.94
  49.1 0.4 collective-permute-start.15
  49.5 9.2 %collective-permute-done.18.refs_0_ = bf16[2,64,512]{2,1,0:T(8,128)(2,1)S(1)} collective-permute-done((bf16[2,64,512]{2,1,0:T(8,128)(2,1)S(1)}, bf16[2,64,512]{2,1,0:T(8,128)(2,1)S(1)}, u32[]{:S(2)}, u32[]{:S(2)}) %collective-permute-start.18) | collective-permute-done | bytes 131104 | tf_op jit(solution)/shard_map/ppermute | solution.py:363
  58.7 1.3 %collective-permute-done.15.refs_1_ = bf16[2,64,512]{2,1,0:T(8,128)(2,1)S(1)} collective-permute-done((bf16[2,64,512]{2,1,0:T(8,128)(2,1)S(1)}, bf16[2,64,512]{2,1,0:T(8,128)(2,1)S(1)}, u32[]{:S(2)}, u32[]{:S(2)}) %collective-permute-start.15) | collective-permute-done | bytes 131104 | tf_op jit(solution)/shard_map/ppermute | solution.py:363
  60.1 0.1 collective-permute-start.20
  60.2 0.0 collective-permute-done.11.got
  60.2 1.0 %shard_map.92 = bf16[1,128,4096]{2,1,0:T(8,128)(2,1)} custom-call(bf16[128,2048]{1,0:T(8,128)(2,1)S(1)} %get-tuple-element.55.mine, bf16[128,2048]{1,0:T(8,128)(2,1)S(1)} %collective-permute-done.11.got), custom_call_target="tpu_custom_call" | custom-call | bytes 524288 | tf_op jit(solution)/shard_map/pallas_call | solution.py:463
  61.2 0.5 collective-permute-done.20.got
  61.7 0.8 %shard_map.98 = (bf16[8,16,1024]{2,1,0:T(8,128)(2,1)}, bf16[8,16,1024]{2,1,0:T(8,128)(2,1)}) custom-call(bf16[2,8,16,512]{3,2,1,0:T(8,128)(2,1)S(1)} %get-tuple-element.69.mine, bf16[2,8,16,512]{3,2,1,0:T(8,128)(2,1)S(1)} %collective-permute-done.20.got), custom_call_target="tpu_custom_call" | custom-call | bytes 524288 | tf_op jit(solution)/shard_map/pallas_call | solution.py:477
  (8 shorter events, 0.1 us)
Async XLA Ops:
  1.8 2.1 %collective-permute-start = (bf16[2,8,16,512]{3,2,1,0:T(8,128)(2,1)S(1)}, bf16[2,8,16,512]{3,2,1,0:T(8,128)(2,1)S(1)}, u32[]{:S(2)}, u32[]{:S(2)}) collective-permute-start(bf16[2,8,16,512]{3,2,1,0:T(8,128)(2,1)S(1)} %get-tuple-element.42), channel_id=1, source_target_pairs={{0,8},{8,0},{16,24},{24,16},{1,9},{9,1},{17,25},{25,17},{2,10},{10... | collective-permute-start | bytes 786440 | tf_op jit(solution)/shard_map/ppermute | solution.py:385
  4.0 8.7 %collective-permute-start.1 = (bf16[272,2048]{1,0:T(8,128)(2,1)S(1)}, bf16[272,2048]{1,0:T(8,128)(2,1)S(1)}, u32[]{:S(2)}, u32[]{:S(2)}) collective-permute-start(bf16[272,2048]{1,0:T(8,128)(2,1)S(1)} %get-tuple-element.44), channel_id=1, source_target_pairs={{0,8},{8,0},{16,24},{24,16},{1,9},{9,1},{17,25},{25,17},{2,10},{10... | collective-permute-start | bytes 3342344 | tf_op jit(solution)/shard_map/ppermute | solution.py:386
  4.1 8.6 %collective-permute-start.2 = (bf16[2,64,512]{2,1,0:T(8,128)(2,1)S(1)}, bf16[2,64,512]{2,1,0:T(8,128)(2,1)S(1)}, u32[]{:S(2)}, u32[]{:S(2)}) collective-permute-start(bf16[2,64,512]{2,1,0:T(8,128)(2,1)S(1)} %get-tuple-element.46), channel_id=1, source_target_pairs={{0,2},{1,3},{2,0},{3,1},{4,6},{5,7},{6,4},{7,5},{8,10},{9,11},{10,... | collective-permute-start | bytes 393224 | tf_op jit(solution)/shard_map/ppermute | solution.py:363
  7.1 12.9 %collective-permute-start.5 = (bf16[2,64,512]{2,1,0:T(8,128)(2,1)S(1)}, bf16[2,64,512]{2,1,0:T(8,128)(2,1)S(1)}, u32[]{:S(2)}, u32[]{:S(2)}) collective-permute-start(bf16[2,64,512]{2,1,0:T(8,128)(2,1)S(1)} %get-tuple-element.49), channel_id=1, source_target_pairs={{0,4},{1,5},{2,6},{3,7},{4,0},{5,1},{6,2},{7,3},{8,12},{9,13},{10,... | collective-permute-start | bytes 393224 | tf_op jit(solution)/shard_map/ppermute | solution.py:363
  9.7 10.3 %collective-permute-start.6 = (bf16[2,64,512]{2,1,0:T(8,128)(2,1)S(1)}, bf16[2,64,512]{2,1,0:T(8,128)(2,1)S(1)}, u32[]{:S(2)}, u32[]{:S(2)}) collective-permute-start(bf16[2,64,512]{2,1,0:T(8,128)(2,1)S(1)} %get-tuple-element.50), channel_id=1, source_target_pairs={{0,6},{1,7},{2,4},{3,5},{4,2},{5,3},{6,0},{7,1},{8,14},{9,15},{10,... | collective-permute-start | bytes 393224 | tf_op jit(solution)/shard_map/ppermute | solution.py:363
  12.7 7.3 %collective-permute-start.3 = (bf16[128,512]{1,0:T(8,128)(2,1)S(1)}, bf16[128,512]{1,0:T(8,128)(2,1)S(1)}, u32[]{:S(2)}, u32[]{:S(2)}) collective-permute-start(bf16[128,512]{1,0:T(8,128)(2,1)S(1)} %get-tuple-element.47.rest_0_), channel_id=1, source_target_pairs={{0,16},{8,24},{16,0},{24,8},{1,17},{9,25},{17,1},{25,9},{2,18},{10... | collective-permute-start | bytes 393224 | tf_op jit(solution)/shard_map/ppermute | solution.py:369
  14.5 5.9 %collective-permute-start.4 = (bf16[128,512]{1,0:T(8,128)(2,1)S(1)}, bf16[128,512]{1,0:T(8,128)(2,1)S(1)}, u32[]{:S(2)}, u32[]{:S(2)}) collective-permute-start(bf16[128,512]{1,0:T(8,128)(2,1)S(1)} %get-tuple-element.48), channel_id=1, source_target_pairs={{0,17},{1,16},{2,19},{3,18},{4,21},{5,20},{6,23},{7,22},{8,25},{9,... | collective-permute-start | bytes 393224 | tf_op jit(solution)/shard_map/ppermute | solution.py:372
  15.9 8.0 %collective-permute-start.9 = (bf16[128,512]{1,0:T(8,128)(2,1)S(1)}, bf16[128,512]{1,0:T(8,128)(2,1)S(1)}, u32[]{:S(2)}, u32[]{:S(2)}) collective-permute-start(bf16[128,512]{1,0:T(8,128)(2,1)S(1)} %get-tuple-element.48), channel_id=1, source_target_pairs={{0,1},{1,0},{2,3},{3,2},{4,5},{5,4},{6,7},{7,6},{8,9},{9,8},{10,11... | collective-permute-start | bytes 393224 | tf_op jit(solution)/shard_map/ppermute | solution.py:366
  20.4 5.5 %collective-permute-start.10 = (bf16[128,512]{1,0:T(8,128)(2,1)S(1)}, bf16[128,512]{1,0:T(8,128)(2,1)S(1)}, u32[]{:S(2)}, u32[]{:S(2)}) collective-permute-start(bf16[128,512]{1,0:T(8,128)(2,1)S(1)} %get-tuple-element.52), channel_id=1, source_target_pairs={{0,1},{1,0},{2,3},{3,2},{4,5},{5,4},{6,7},{7,6},{8,9},{9,8},{10,11... | collective-permute-start | bytes 393224 | tf_op jit(solution)/shard_map/ppermute | solution.py:366
  22.0 8.2 %collective-permute-start.7 = (bf16[128,512]{1,0:T(8,128)(2,1)S(1)}, bf16[128,512]{1,0:T(8,128)(2,1)S(1)}, u32[]{:S(2)}, u32[]{:S(2)}) collective-permute-start(bf16[128,512]{1,0:T(8,128)(2,1)S(1)} %get-tuple-element.51.rest_2_), channel_id=1, source_target_pairs={{0,16},{8,24},{16,0},{24,8},{1,17},{9,25},{17,1},{25,9},{2,18},{10... | collective-permute-start | bytes 393224 | tf_op jit(solution)/shard_map/ppermute | solution.py:369
  23.1 8.1 %collective-permute-start.8 = (bf16[128,512]{1,0:T(8,128)(2,1)S(1)}, bf16[128,512]{1,0:T(8,128)(2,1)S(1)}, u32[]{:S(2)}, u32[]{:S(2)}) collective-permute-start(bf16[128,512]{1,0:T(8,128)(2,1)S(1)} %get-tuple-element.52), channel_id=1, source_target_pairs={{0,17},{1,16},{2,19},{3,18},{4,21},{5,20},{6,23},{7,22},{8,25},{9,... | collective-permute-start | bytes 393224 | tf_op jit(solution)/shard_map/ppermute | solution.py:372
  30.2 13.3 %collective-permute-start.12 = (bf16[256,512]{1,0:T(8,128)(2,1)S(1)}, bf16[256,512]{1,0:T(8,128)(2,1)S(1)}, u32[]{:S(2)}, u32[]{:S(2)}) collective-permute-start(bf16[256,512]{1,0:T(8,128)(2,1)S(1)} %shard_map.93), channel_id=1, source_target_pairs={{0,1},{1,0},{2,3},{3,2},{4,5},{5,4},{6,7},{7,6},{8,9},{9,8},{10,11... | collective-permute-start | bytes 786440 | tf_op jit(solution)/shard_map/ppermute | solution.py:366
  31.5 12.0 %collective-permute-start.16 = (bf16[128,512]{1,0:T(8,128)(2,1)S(1)}, bf16[128,512]{1,0:T(8,128)(2,1)S(1)}, u32[]{:S(2)}, u32[]{:S(2)}) collective-permute-start(bf16[128,512]{1,0:T(8,128)(2,1)S(1)} %get-tuple-element.63), channel_id=1, source_target_pairs={{0,16},{8,24},{16,0},{24,8},{1,17},{9,25},{17,1},{25,9},{2,18},{10... | collective-permute-start | bytes 393224 | tf_op jit(solution)/shard_map/ppermute | solution.py:369
  36.9 6.6 %collective-permute-start.17 = (bf16[128,512]{1,0:T(8,128)(2,1)S(1)}, bf16[128,512]{1,0:T(8,128)(2,1)S(1)}, u32[]{:S(2)}, u32[]{:S(2)}) collective-permute-start(bf16[128,512]{1,0:T(8,128)(2,1)S(1)} %get-tuple-element.64), channel_id=1, source_target_pairs={{0,17},{1,16},{2,19},{3,18},{4,21},{5,20},{6,23},{7,22},{8,25},{9,... | collective-permute-start | bytes 393224 | tf_op jit(solution)/shard_map/ppermute | solution.py:372
  37.7 11.4 %collective-permute-start.13 = (bf16[128,512]{1,0:T(8,128)(2,1)S(1)}, bf16[128,512]{1,0:T(8,128)(2,1)S(1)}, u32[]{:S(2)}, u32[]{:S(2)}) collective-permute-start(bf16[128,512]{1,0:T(8,128)(2,1)S(1)} %get-tuple-element.59), channel_id=1, source_target_pairs={{0,16},{8,24},{16,0},{24,8},{1,17},{9,25},{17,1},{25,9},{2,18},{10... | collective-permute-start | bytes 393224 | tf_op jit(solution)/shard_map/ppermute | solution.py:369
  39.6 9.5 %collective-permute-start.14 = (bf16[128,512]{1,0:T(8,128)(2,1)S(1)}, bf16[128,512]{1,0:T(8,128)(2,1)S(1)}, u32[]{:S(2)}, u32[]{:S(2)}) collective-permute-start(bf16[128,512]{1,0:T(8,128)(2,1)S(1)} %get-tuple-element.60), channel_id=1, source_target_pairs={{0,17},{1,16},{2,19},{3,18},{4,21},{5,20},{6,23},{7,22},{8,25},{9,... | collective-permute-start | bytes 393224 | tf_op jit(solution)/shard_map/ppermute | solution.py:372
  43.5 16.7 %collective-permute-start.11 = (bf16[128,2048]{1,0:T(8,128)(2,1)S(1)}, bf16[128,2048]{1,0:T(8,128)(2,1)S(1)}, u32[]{:S(2)}, u32[]{:S(2)}) collective-permute-start(bf16[128,2048]{1,0:T(8,128)(2,1)S(1)} %get-tuple-element.56), channel_id=1, source_target_pairs={{0,8},{8,0},{16,24},{24,16},{1,9},{9,1},{17,25},{25,17},{2,10},{10... | collective-permute-start | bytes 1572872 | tf_op jit(solution)/shard_map/ppermute | solution.py:404
  43.6 15.1 %collective-permute-start.18 = (bf16[2,64,512]{2,1,0:T(8,128)(2,1)S(1)}, bf16[2,64,512]{2,1,0:T(8,128)(2,1)S(1)}, u32[]{:S(2)}, u32[]{:S(2)}) collective-permute-start(bf16[2,64,512]{2,1,0:T(8,128)(2,1)S(1)} %get-tuple-element.65), channel_id=1, source_target_pairs={{0,4},{1,5},{2,6},{3,7},{4,0},{5,1},{6,2},{7,3},{8,12},{9,13},{10,... | collective-permute-start | bytes 393224 | tf_op jit(solution)/shard_map/ppermute | solution.py:363
  48.8 9.9 %collective-permute-start.19 = (bf16[2,64,512]{2,1,0:T(8,128)(2,1)S(1)}, bf16[2,64,512]{2,1,0:T(8,128)(2,1)S(1)}, u32[]{:S(2)}, u32[]{:S(2)}) collective-permute-start(bf16[2,64,512]{2,1,0:T(8,128)(2,1)S(1)} %get-tuple-element.66), channel_id=1, source_target_pairs={{0,6},{1,7},{2,4},{3,5},{4,2},{5,3},{6,0},{7,1},{8,14},{9,15},{10,... | collective-permute-start | bytes 393224 | tf_op jit(solution)/shard_map/ppermute | solution.py:363
  49.1 10.9 %collective-permute-start.15 = (bf16[2,64,512]{2,1,0:T(8,128)(2,1)S(1)}, bf16[2,64,512]{2,1,0:T(8,128)(2,1)S(1)}, u32[]{:S(2)}, u32[]{:S(2)}) collective-permute-start(bf16[2,64,512]{2,1,0:T(8,128)(2,1)S(1)} %get-tuple-element.62), channel_id=1, source_target_pairs={{0,2},{1,3},{2,0},{3,1},{4,6},{5,7},{6,4},{7,5},{8,10},{9,11},{10,... | collective-permute-start | bytes 393224 | tf_op jit(solution)/shard_map/ppermute | solution.py:363
  60.1 1.6 %collective-permute-start.20 = (bf16[2,8,16,512]{3,2,1,0:T(8,128)(2,1)S(1)}, bf16[2,8,16,512]{3,2,1,0:T(8,128)(2,1)S(1)}, u32[]{:S(2)}, u32[]{:S(2)}) collective-permute-start(bf16[2,8,16,512]{3,2,1,0:T(8,128)(2,1)S(1)} %get-tuple-element.70), channel_id=1, source_target_pairs={{0,8},{8,0},{16,24},{24,16},{1,9},{9,1},{17,25},{25,17},{2,10},{10... | collective-permute-start | bytes 786440 | tf_op jit(solution)/shard_map/ppermute | solution.py:482
where the time goes:
time: 62.3 us; the launch traced here: 62.5 us
  starting transfers between devices  28.8 us (46%)
  waiting for transfers between devices  23.7 us (38%)
  Pallas kernels  9.3 us (15%)
  between operations  0.77 us (1%)
    ppermute x6, waiting for transfers between devices, along_z(): lax.ppermute(part, 'enc', [(i, i ^ 2 * dz) for i in range(n_enc)])  17.2 us
    ppermute x6, starting transfers between devices, along_z(): lax.ppermute(part, 'enc', [(i, i ^ 2 * dz) for i in range(n_enc)])  11.5 us
    ppermute x4, starting transfers between devices, along_y(): return lax.ppermute(part, 'ctx', swap_y)  10.3 us
    pallas_call x10, Pallas kernels, call(): return local_call(body, [IN_VMEM] * len(args), spec, **more)(*args)  4.75 us
    ppermute x4, waiting for transfers between devices, along_y(): return lax.ppermute(part, 'ctx', swap_y)  3.63 us
    ppermute x4, starting transfers between devices, along_xy(): return lax.ppermute(part, ('ctx', 'enc'), swap_xy)  3.29 us
    ppermute x3, starting transfers between devices, along_x(): return lax.ppermute(part, 'enc', swap_x)  2.97 us
    ppermute x3, waiting for transfers between devices, along_x(): return lax.ppermute(part, 'enc', swap_x)  1.93 us
  transfers between devices with their start and end apart: 21, of which 8 were waited for; matrix products, arithmetic and copies ran while one was open for 0% of the time, Pallas kernels for 12%

commit v1 on v0

--- a/solution.py
+++ b/solution.py
@@ -21,6 +21,8 @@
 HALF_QCOLS = HALF_KCOLS * RATIO
 WIDE = RATIO * HD
 SAMP_ROWS = 16
+TILE = 256
+DQ_PARTS = 2
 SCALE = HD ** (-0.5)
 LOG2E = 1.4426950408889634
 BIG_NEGATIVE = -1e30
@@ -206,7 +208,7 @@
                     out[i, enc ^ (2 * len(parts) + d)] = from_far[i, d]
 
 
-def finish_kernel(mine, got, dk, dv, sems):
+def finish_kernel(mine, got, _, dk, dv, sems):
     core = core_of()
     pairs = []
     for half, ref in ((core, mine), (1 - core, got)):
@@ -216,11 +218,23 @@
     run_copies(pairs, sems)
 
 
-def finish_text_kernel(mine, got, out, sems):
-    core = core_of()
-    pairs = []
-    for half, ref in ((core, mine), (1 - core, got)):
-        pairs.append((ref, out.at[0, :, at_cols(half * HALF_QCOLS, HALF_QCOLS, HALF_QCOLS)]))
+def split_rows_kernel(whole, *refs):
+    outs = refs[-DQ_PARTS:]
+    rows = outs[0].shape[0]
+    for i, out in enumerate(outs):
+        out[...] = whole[i * rows : (i + 1) * rows, :]
+
+
+def finish_text_kernel(mine, *refs):
+    got, (out, token, sems) = refs[:-3], refs[-3:]
+    core = core_of()
+    token[...] = jnp.zeros_like(token)
+    own_cols = at_cols(core * HALF_QCOLS, HALF_QCOLS, HALF_QCOLS)
+    got_cols = at_cols((1 - core) * HALF_QCOLS, HALF_QCOLS, HALF_QCOLS)
+    pairs = [(mine, out.at[0, :, own_cols])]
+    rows = got[0].shape[0]
+    for i, ref in enumerate(got):
+        pairs.append((ref, out.at[0, i * rows : (i + 1) * rows, got_cols]))
     run_copies(pairs, sems)
 
 
@@ -230,7 +244,7 @@
     if with_prev:
         prev, rest = rest[:2], rest[2:]
     rest = rest[n_through:]
-    dqs, grads = rest[:2], rest[2 : 2 + n_grads]
+    dqs, grads, (ds_all, ph_all) = rest[:2], rest[2 : 2 + n_grads], rest[-2:]
     sample = where()[0] ^ role
     tokens = g_a.shape[0]
     block_rows = SLOT_ROWS // n_blocks
@@ -246,6 +260,7 @@
         for h in range(HALF_KV):
             first_q = h * WIDE
             first_k = h * HD
+            ds_ref, ph_ref = ds_all.at[h % 2], ph_all.at[h % 2]
 
             def stacked(ref_a, first_b):
                 parts = [
@@ -266,16 +281,23 @@
             g = stacked(g_a, tokens)
             k = rows_of(0)
             v = rows_of(block_rows)
-            s = lax.dot_general(k, q, NT, preferred_element_type=F32)
-            s = s + jnp.concatenate([bias[role]] * (s.shape[1] // HD), axis=1)
-            top = jnp.max(s, axis=0, keepdims=True)
-            e = jnp.exp2((s - top) * (SCALE * LOG2E))
-            total = jnp.sum(e, axis=0, keepdims=True)
-            p = e * jnp.where(mine, 1.0 / total, 0.0)
-            gp = lax.dot_general(v, g, NT, preferred_element_type=F32)
-            row_dot = jnp.sum(p * gp, axis=0, keepdims=True)
-            ds = (p * (gp - row_dot)).astype(BF16)
-            dv = jnp.dot(p.astype(BF16), g, preferred_element_type=F32)
+            for first in range(0, q.shape[0], TILE):
+                many = slice(first, first + TILE)
+                s = lax.dot_general(k, q[many], NT, preferred_element_type=F32)
+                gp = lax.dot_general(v, g[many], NT, preferred_element_type=F32)
+                for at in range(0, TILE, HD):
+                    one = slice(at, at + HD)
+                    here = slice(first + at, first + at + HD)
+                    part = s[:, one] + bias[role]
+                    top = jnp.max(part, axis=0, keepdims=True)
+                    e = jnp.exp2((part - top) * (SCALE * LOG2E))
+                    total = jnp.sum(e, axis=0, keepdims=True)
+                    p = e * jnp.where(mine[:, here], 1.0 / total, 0.0)
+                    row_dot = jnp.sum(p * gp[:, one], axis=0, keepdims=True)
+                    ds_ref[:, here] = (p * (gp[:, one] - row_dot)).astype(BF16)
+                    ph_ref[:, here] = p.astype(BF16)
+            ds = ds_ref[...]
+            dv = jnp.dot(ph_ref[...], g, preferred_element_type=F32)
             dk = jnp.dot(ds, q, preferred_element_type=F32) * SCALE
             dq = lax.dot_general(ds, k, TN, preferred_element_type=F32) * SCALE
             for t, dq_ref in enumerate(dqs):
@@ -311,6 +333,7 @@
             pass_kernel, role, n_blocks, len(kvs), prev is not None, len(through), len(grads), where
         ),
         [dq, dq, *grads] + [(a.shape, a.dtype) for a in through],
+        scratch=[pltpu.VMEM((2, SLOT_ROWS, CORES * RATIO * tokens), BF16)] * 2,
         flops=10 * tokens * WIDE * SLOT_ROWS * CORES * HALF_KV,
         moved=16 * 2**20,
         aliases={len(args) + i: 2 + len(grads) + i for i in range(len(through))},
@@ -401,15 +424,21 @@
         dq, far_grads = sample_pass(
             near_place, 1, n_enc, bias, text, far, own_dq, [(quarter, BF16)] * 4
         )
-        dq_got = lax.ppermute(dq[1], "ctx", swap_core)
         returned = [None] * n_z
         for z in (2, 0):
             here, beside = far_grads[z : z + 2]
+            back_y = along_y(here)
             totals = in_vmem(functools.partial(add_kernel, z), [(pair, BF16)] * 2)(
-                own_here, back_x, along_y(here), along_xy(beside)
+                own_here, back_x, back_y, along_xy(beside)
             )
             for dz, total in enumerate(totals, z):
                 returned[dz] = along_z(total, dz)
+            if z:
+                sent = totals[0]
+        dq_parts = in_vmem(split_rows_kernel, [((tokens // DQ_PARTS, HALF_QCOLS), BF16)] * DQ_PARTS)(
+            dq[1], sent, totals[0]
+        )
+        dq_got = [lax.ppermute(part, "ctx", swap_core) for part in dq_parts]
     else:
         both = ("ctx", "enc")
         same_y = [
@@ -458,28 +487,29 @@
             grads += grad
         d_img_k = to_owners(jnp.concatenate([g[:SLOT_ROWS] for g in grads], axis=0))
         d_img_v = to_owners(jnp.concatenate([g[SLOT_ROWS:] for g in grads], axis=0))
-        dq_got = lax.ppermute(dq[1], "ctx", swap_core)
-
-    (d_queries,) = local_call(
+        dq_got = [lax.ppermute(dq[1], "ctx", swap_core)]
+
+    d_queries, token = local_call(
         finish_text_kernel,
-        [IN_VMEM] * 2,
-        [(queries.shape, BF16, IN_HBM)],
-        [pltpu.SemaphoreType.DMA((2,))],
-    )(dq[0], dq_got)
+        [IN_VMEM] * (1 + len(dq_got)),
+        [(queries.shape, BF16, IN_HBM), ((8, HD), F32, IN_VMEM)],
+        [pltpu.SemaphoreType.DMA((1 + len(dq_got),))],
+    )(dq[0], *dq_got)
     if near:
         far_rows = in_vmem(
             functools.partial(far_rows_kernel, slots),
             [((2, n_enc // 2, slots, HALF_KCOLS), BF16)] * 2,
         )(*returned[2:])
         mine, for_peer = in_vmem(
-            functools.partial(owner_rows_kernel, slots), [(kv_halves, BF16)] * 2
+            functools.partial(owner_rows_kernel, slots),
+            [(kv_halves, BF16)] * 2,
         )(*returned[:2], *far_rows)
         d_img_k, d_img_v = local_call(
             finish_kernel,
-            [IN_VMEM] * 2,
+            [IN_VMEM] * 3,
             [(img_k.shape, BF16, IN_HBM)] * 2,
             [pltpu.SemaphoreType.DMA((4,))],
-        )(mine, lax.ppermute(for_peer, "ctx", swap_core))
+        )(mine, lax.ppermute(for_peer, "ctx", swap_core), token)
     return (d_queries, d_img_k, d_img_v)
 
 

time: 62.3 us -> 60.2 us (0.966)
  waiting for transfers between devices: 23.7 us -> 19.9 us
  Pallas kernels: 9.3 us -> 10.3 us
    ppermute x6, waiting for transfers between devices: 17.2 us -> 12.4 us  [along_z(): lax.ppermute(part, 'enc', [(i, i ^ 2 * dz) for i in range(n_enc)])]
    ppermute x4, starting transfers between devices: 3.29 us -> 5.16 us  [along_xy(): return lax.ppermute(part, ('ctx', 'enc'), swap_xy)]
    ppermute x6, starting transfers between devices: 11.5 us -> 10.3 us  [along_z(): lax.ppermute(part, 'enc', [(i, i ^ 2 * dz) for i in range(n_enc)])]
    ppermute x4, waiting for transfers between devices: 3.63 us -> 4.72 us  [along_y(): return lax.ppermute(part, 'ctx', swap_y)]
    ppermute x4, starting transfers between devices: 10.3 us -> 9.31 us  [along_y(): return lax.ppermute(part, 'ctx', swap_y)]
    pallas_call x10 -> x11, Pallas kernels: 4.75 us -> 5.7 us  [call(): return local_call(body, [IN_VMEM] * len(args), spec, **more)(*args)]
  transfers between devices with their start and end apart: 21 -> 22, of which waited for: 8 -> 8; matrix products, arithmetic and copies ran while one was open for 0% -> 0% of each run, Pallas kernels for 12% -> 14%
where the time goes in v1:
time: 60.2 us; the launch traced here: 60 us
  starting transfers between devices  29.1 us (48%)
  waiting for transfers between devices  19.9 us (33%)
  Pallas kernels  10.3 us (17%)
  between operations  0.79 us (1%)
    ppermute x6, waiting for transfers between devices, along_z(): lax.ppermute(part, 'enc', [(i, i ^ 2 * dz) for i in range(n_enc)])  12.4 us
    ppermute x6, starting transfers between devices, along_z(): lax.ppermute(part, 'enc', [(i, i ^ 2 * dz) for i in range(n_enc)])  10.3 us
    ppermute x4, starting transfers between devices, along_y(): return lax.ppermute(part, 'ctx', swap_y)  9.31 us
    pallas_call x11, Pallas kernels, call(): return local_call(body, [IN_VMEM] * len(args), spec, **more)(*args)  5.7 us
    ppermute x4, starting transfers between devices, along_xy(): return lax.ppermute(part, ('ctx', 'enc'), swap_xy)  5.16 us
    ppermute x4, waiting for transfers between devices, along_y(): return lax.ppermute(part, 'ctx', swap_y)  4.72 us
    ppermute x3, starting transfers between devices, along_x(): return lax.ppermute(part, 'enc', swap_x)  2.97 us
    ppermute x3, waiting for transfers between devices, along_x(): return lax.ppermute(part, 'enc', swap_x)  1.93 us
  transfers between devices with their start and end apart: 22, of which 8 were waited for; matrix products, arithmetic and copies ran while one was open for 0% of the time, Pallas kernels for 14%

profile of v1, /device:TPU:0, one launch (start us, length us, event | category | flops | bytes accessed | tf_op | source)
XLA Modules:
  0.0 60.0 jit_solution(11716617664560528525)
XLA Ops:
  0.6 1.1 %shard_map.86 = (bf16[2,8,16,512]{3,2,1,0:T(8,128)(2,1)S(1)}, bf16[2,8,16,512]{3,2,1,0:T(8,128)(2,1)S(1)}) custom-call(bf16[8,16,1024]{2,1,0:T(8,128)(2,1)} %k_ref.1, bf16[8,16,1024]{2,1,0:T(8,128)(2,1)} %v_ref.1), custom_call_target="tpu_custom_call" | custom-call | bytes 524288 | tf_op jit(solution)/shard_map/pallas_call | solution.py:397
  1.8 0.5 collective-permute-start
  2.3 1.6 %shard_map.85 = (bf16[272,2048]{1,0:T(8,128)(2,1)S(1)}, bf16[144,2048]{1,0:T(8,128)(2,1)S(1)}, bf16[128,2048]{1,0:T(8,128)(2,1)S(1)}, f32[2,256,128]{2,1,0:T(8,128)S(1)}) custom-call(bf16[1,128,4096]{2,1,0:T(8,128)(2,1)} %q_ref.1, bf16[1,128,4096]{2,1,0:T(8,128)(2,1)} %g_ref.1, s32[1,128]{1,0:T(1,128)} %samp_hbm.1, s32[1,2]{1,0:T(1,128)} %tiles_hbm.1), custom_call_target="tpu_custom_call" | custom-call | bytes 4194304 | tf_op jit(solution)/shard_map/pallas_call | solution.py:358
  3.9 0.0 collective-permute-done.got
  3.9 0.1 shard_map.87
  4.0 0.1 collective-permute-start.1
  4.1 3.0 %collective-permute-start.2 = (bf16[2,64,512]{2,1,0:T(8,128)(2,1)S(1)}, bf16[2,64,512]{2,1,0:T(8,128)(2,1)S(1)}, u32[]{:S(2)}, u32[]{:S(2)}) collective-permute-start(bf16[2,64,512]{2,1,0:T(8,128)(2,1)S(1)} %get-tuple-element.50), channel_id=1, source_target_pairs={{0,2},{1,3},{2,0},{3,1},{4,6},{5,7},{6,4},{7,5},{8,10},{9,11},{10,... | collective-permute-start | bytes 393224 | tf_op jit(solution)/shard_map/ppermute | solution.py:386
  7.1 2.6 %collective-permute-start.5 = (bf16[2,64,512]{2,1,0:T(8,128)(2,1)S(1)}, bf16[2,64,512]{2,1,0:T(8,128)(2,1)S(1)}, u32[]{:S(2)}, u32[]{:S(2)}) collective-permute-start(bf16[2,64,512]{2,1,0:T(8,128)(2,1)S(1)} %get-tuple-element.53), channel_id=1, source_target_pairs={{0,4},{1,5},{2,6},{3,7},{4,0},{5,1},{6,2},{7,3},{8,12},{9,13},{10,... | collective-permute-start | bytes 393224 | tf_op jit(solution)/shard_map/ppermute | solution.py:386
  9.7 0.0 collective-permute-start.6
  9.7 3.0 %collective-permute-done.2.refs_1_ = bf16[2,64,512]{2,1,0:T(8,128)(2,1)S(1)} collective-permute-done((bf16[2,64,512]{2,1,0:T(8,128)(2,1)S(1)}, bf16[2,64,512]{2,1,0:T(8,128)(2,1)S(1)}, u32[]{:S(2)}, u32[]{:S(2)}) %collective-permute-start.2) | collective-permute-done | bytes 131104 | tf_op jit(solution)/shard_map/ppermute | solution.py:386
  12.7 0.0 collective-permute-done.1.refs_2_.got
  12.7 1.8 %collective-permute-start.3 = (bf16[128,512]{1,0:T(8,128)(2,1)S(1)}, bf16[128,512]{1,0:T(8,128)(2,1)S(1)}, u32[]{:S(2)}, u32[]{:S(2)}) collective-permute-start(bf16[128,512]{1,0:T(8,128)(2,1)S(1)} %get-tuple-element.51.rest_0_), channel_id=1, source_target_pairs={{0,16},{8,24},{16,0},{24,8},{1,17},{9,25},{17,1},{25,9},{2,18},{10... | collective-permute-start | bytes 393224 | tf_op jit(solution)/shard_map/ppermute | solution.py:392
  14.5 1.4 %collective-permute-start.4 = (bf16[128,512]{1,0:T(8,128)(2,1)S(1)}, bf16[128,512]{1,0:T(8,128)(2,1)S(1)}, u32[]{:S(2)}, u32[]{:S(2)}) collective-permute-start(bf16[128,512]{1,0:T(8,128)(2,1)S(1)} %get-tuple-element.52), channel_id=1, source_target_pairs={{0,17},{1,16},{2,19},{3,18},{4,21},{5,20},{6,23},{7,22},{8,25},{9,... | collective-permute-start | bytes 393224 | tf_op jit(solution)/shard_map/ppermute | solution.py:395
  15.9 0.3 collective-permute-start.9
  16.3 3.8 %collective-permute-done.5.refs_0_ = bf16[2,64,512]{2,1,0:T(8,128)(2,1)S(1)} collective-permute-done((bf16[2,64,512]{2,1,0:T(8,128)(2,1)S(1)}, bf16[2,64,512]{2,1,0:T(8,128)(2,1)S(1)}, u32[]{:S(2)}, u32[]{:S(2)}) %collective-permute-start.5) | collective-permute-done | bytes 131104 | tf_op jit(solution)/shard_map/ppermute | solution.py:386
  20.0 0.0 collective-permute-done.6.refs_1_
  20.0 0.3 collective-permute-done.4.refs_4_.rest_1_
  20.4 1.6 %collective-permute-start.10 = (bf16[128,512]{1,0:T(8,128)(2,1)S(1)}, bf16[128,512]{1,0:T(8,128)(2,1)S(1)}, u32[]{:S(2)}, u32[]{:S(2)}) collective-permute-start(bf16[128,512]{1,0:T(8,128)(2,1)S(1)} %get-tuple-element.56), channel_id=1, source_target_pairs={{0,1},{1,0},{2,3},{3,2},{4,5},{5,4},{6,7},{7,6},{8,9},{9,8},{10,11... | collective-permute-start | bytes 393224 | tf_op jit(solution)/shard_map/ppermute | solution.py:389
  22.0 1.2 %collective-permute-start.7 = (bf16[128,512]{1,0:T(8,128)(2,1)S(1)}, bf16[128,512]{1,0:T(8,128)(2,1)S(1)}, u32[]{:S(2)}, u32[]{:S(2)}) collective-permute-start(bf16[128,512]{1,0:T(8,128)(2,1)S(1)} %get-tuple-element.55.rest_2_), channel_id=1, source_target_pairs={{0,16},{8,24},{16,0},{24,8},{1,17},{9,25},{17,1},{25,9},{2,18},{10... | collective-permute-start | bytes 393224 | tf_op jit(solution)/shard_map/ppermute | solution.py:392
  23.1 0.8 %collective-permute-start.8 = (bf16[128,512]{1,0:T(8,128)(2,1)S(1)}, bf16[128,512]{1,0:T(8,128)(2,1)S(1)}, u32[]{:S(2)}, u32[]{:S(2)}) collective-permute-start(bf16[128,512]{1,0:T(8,128)(2,1)S(1)} %get-tuple-element.56), channel_id=1, source_target_pairs={{0,17},{1,16},{2,19},{3,18},{4,21},{5,20},{6,23},{7,22},{8,25},{9,... | collective-permute-start | bytes 393224 | tf_op jit(solution)/shard_map/ppermute | solution.py:395
  24.0 1.9 %collective-permute-done.10.rest_3_ = bf16[128,512]{1,0:T(8,128)(2,1)S(1)} collective-permute-done((bf16[128,512]{1,0:T(8,128)(2,1)S(1)}, bf16[128,512]{1,0:T(8,128)(2,1)S(1)}, u32[]{:S(2)}, u32[]{:S(2)}) %collective-permute-start.10) | collective-permute-done | bytes 131104 | tf_op jit(solution)/shard_map/ppermute | solution.py:389
  25.9 5.2 %shard_map.90 = (bf16[128,2048]{1,0:T(8,128)(2,1)S(1)}, bf16[128,2048]{1,0:T(8,128)(2,1)S(1)}, f32[256,512]{1,0:T(8,128)S(1)}, bf16[256,512]{1,0:T(8,128)(2,1)S(1)}) custom-call(f32[2,256,128]{2,1,0:T(8,128)S(1)} %get-tuple-element.42.bias, bf16[144,2048]{1,0:T(8,128)(2,1)S(1)} %get-tuple-element.43.q_a, bf16[128,2048]{1,0:T(8,128)(2,1)S(1)} %get-tuple-element.44.g_a, ...), custom_call_target="tpu_custom_call" | custom-call | flops 1342177280 | bytes 16777216 | tf_op jit(solution)/shard_map/pallas_call | solution.py:56
  31.1 0.0 collective-permute-done.7.rest_2_.refs_1_
  31.1 1.1 %collective-permute-start.11 = (bf16[256,512]{1,0:T(8,128)(2,1)S(1)}, bf16[256,512]{1,0:T(8,128)(2,1)S(1)}, u32[]{:S(2)}, u32[]{:S(2)}) collective-permute-start(bf16[256,512]{1,0:T(8,128)(2,1)S(1)} %shard_map.92), channel_id=1, source_target_pairs={{0,1},{1,0},{2,3},{3,2},{4,5},{5,4},{6,7},{7,6},{8,9},{9,8},{10,11... | collective-permute-start | bytes 786440 | tf_op jit(solution)/shard_map/ppermute | solution.py:389
  32.2 0.0 collective-permute-done.8.rest_3_
  32.2 0.2 shard_map.91
  32.4 6.2 %collective-permute-start.12 = (bf16[128,512]{1,0:T(8,128)(2,1)S(1)}, bf16[128,512]{1,0:T(8,128)(2,1)S(1)}, u32[]{:S(2)}, u32[]{:S(2)}) collective-permute-start(bf16[128,512]{1,0:T(8,128)(2,1)S(1)} %get-tuple-element.63), channel_id=1, source_target_pairs={{0,16},{8,24},{16,0},{24,8},{1,17},{9,25},{17,1},{25,9},{2,18},{10... | collective-permute-start | bytes 393224 | tf_op jit(solution)/shard_map/ppermute | solution.py:392
  38.7 1.3 %collective-permute-start.13 = (bf16[128,512]{1,0:T(8,128)(2,1)S(1)}, bf16[128,512]{1,0:T(8,128)(2,1)S(1)}, u32[]{:S(2)}, u32[]{:S(2)}) collective-permute-start(bf16[128,512]{1,0:T(8,128)(2,1)S(1)} %get-tuple-element.64), channel_id=1, source_target_pairs={{0,17},{1,16},{2,19},{3,18},{4,21},{5,20},{6,23},{7,22},{8,25},{9,... | collective-permute-start | bytes 393224 | tf_op jit(solution)/shard_map/ppermute | solution.py:395
  39.9 0.1 collective-permute-start.14
  40.0 1.7 %collective-permute-start.15 = (bf16[128,512]{1,0:T(8,128)(2,1)S(1)}, bf16[128,512]{1,0:T(8,128)(2,1)S(1)}, u32[]{:S(2)}, u32[]{:S(2)}) collective-permute-start(bf16[128,512]{1,0:T(8,128)(2,1)S(1)} %get-tuple-element.67), channel_id=1, source_target_pairs={{0,17},{1,16},{2,19},{3,18},{4,21},{5,20},{6,23},{7,22},{8,25},{9,... | collective-permute-start | bytes 393224 | tf_op jit(solution)/shard_map/ppermute | solution.py:395
  41.7 4.7 %collective-permute-done.12.back_y = bf16[128,512]{1,0:T(8,128)(2,1)S(1)} collective-permute-done((bf16[128,512]{1,0:T(8,128)(2,1)S(1)}, bf16[128,512]{1,0:T(8,128)(2,1)S(1)}, u32[]{:S(2)}, u32[]{:S(2)}) %collective-permute-start.12) | collective-permute-done | bytes 131104 | tf_op jit(solution)/shard_map/ppermute | solution.py:392
  46.4 0.0 collective-permute-done.13.back_xy
  46.4 0.1 shard_map.93
  46.4 2.9 %collective-permute-start.20 = (bf16[2,64,512]{2,1,0:T(8,128)(2,1)S(1)}, bf16[2,64,512]{2,1,0:T(8,128)(2,1)S(1)}, u32[]{:S(2)}, u32[]{:S(2)}) collective-permute-start(bf16[2,64,512]{2,1,0:T(8,128)(2,1)S(1)} %get-tuple-element.73), channel_id=1, source_target_pairs={{0,6},{1,7},{2,4},{3,5},{4,2},{5,3},{6,0},{7,1},{8,14},{9,15},{10,... | collective-permute-start | bytes 393224 | tf_op jit(solution)/shard_map/ppermute | solution.py:386
  49.3 1.6 %collective-permute-start.19 = (bf16[2,64,512]{2,1,0:T(8,128)(2,1)S(1)}, bf16[2,64,512]{2,1,0:T(8,128)(2,1)S(1)}, u32[]{:S(2)}, u32[]{:S(2)}) collective-permute-start(bf16[2,64,512]{2,1,0:T(8,128)(2,1)S(1)} %get-tuple-element.65.refs_0_), channel_id=1, source_target_pairs={{0,4},{1,5},{2,6},{3,7},{4,0},{5,1},{6,2},{7,3},{8,12},{9,13},{10,... | collective-permute-start | bytes 393224 | tf_op jit(solution)/shard_map/ppermute | solution.py:386
  50.9 0.1 shard_map.94
  51.0 0.2 collective-permute-start.18
  51.2 0.1 collective-permute-start.16
  51.3 0.5 collective-permute-start.17
  51.8 2.3 %collective-permute-done.20.refs_1_ = bf16[2,64,512]{2,1,0:T(8,128)(2,1)S(1)} collective-permute-done((bf16[2,64,512]{2,1,0:T(8,128)(2,1)S(1)}, bf16[2,64,512]{2,1,0:T(8,128)(2,1)S(1)}, u32[]{:S(2)}, u32[]{:S(2)}) %collective-permute-start.20) | collective-permute-done | bytes 131104 | tf_op jit(solution)/shard_map/ppermute | solution.py:386
  54.1 3.4 %collective-permute-done.19.refs_0_ = bf16[2,64,512]{2,1,0:T(8,128)(2,1)S(1)} collective-permute-done((bf16[2,64,512]{2,1,0:T(8,128)(2,1)S(1)}, bf16[2,64,512]{2,1,0:T(8,128)(2,1)S(1)}, u32[]{:S(2)}, u32[]{:S(2)}) %collective-permute-start.19) | collective-permute-done | bytes 131104 | tf_op jit(solution)/shard_map/ppermute | solution.py:386
  57.5 0.0 collective-permute-done.18.refs_1_
  57.5 0.1 shard_map.98
  57.6 0.1 collective-permute-start.21
  57.6 0.0 collective-permute-done.16.refs_0_
  57.7 1.0 %shard_map.96 = (bf16[1,128,4096]{2,1,0:T(8,128)(2,1)}, f32[8,128]{1,0:T(8,128)S(1)}) custom-call(bf16[128,2048]{1,0:T(8,128)(2,1)S(1)} %get-tuple-element.59.mine, bf16[64,2048]{1,0:T(8,128)(2,1)S(1)} %collective-permute-done.16.refs_0_, bf16[64,2048]{1,0:T(8,128)(2,1)S(1)} %collective-permute-done.17.refs_1_), custom_call_target="tpu_custom_call" | custom-call | bytes 524288 | tf_op jit(solution)/shard_map/pallas_call | solution.py:492
  58.7 0.5 collective-permute-done.21.got
  59.2 0.8 %shard_map.99 = (bf16[8,16,1024]{2,1,0:T(8,128)(2,1)}, bf16[8,16,1024]{2,1,0:T(8,128)(2,1)}) custom-call(bf16[2,8,16,512]{3,2,1,0:T(8,128)(2,1)S(1)} %get-tuple-element.76.mine, bf16[2,8,16,512]{3,2,1,0:T(8,128)(2,1)S(1)} %collective-permute-done.21.got, f32[8,128]{1,0:T(8,128)S(1)} %get-tuple-element.78._), custom_call_target="tpu_custom_call" | custom-call | bytes 524288 | tf_op jit(solution)/shard_map/pallas_call | solution.py:507
  (11 shorter events, 0.1 us)
Async XLA Ops:
  1.8 2.1 %collective-permute-start = (bf16[2,8,16,512]{3,2,1,0:T(8,128)(2,1)S(1)}, bf16[2,8,16,512]{3,2,1,0:T(8,128)(2,1)S(1)}, u32[]{:S(2)}, u32[]{:S(2)}) collective-permute-start(bf16[2,8,16,512]{3,2,1,0:T(8,128)(2,1)S(1)} %get-tuple-element.46), channel_id=1, source_target_pairs={{0,8},{8,0},{16,24},{24,16},{1,9},{9,1},{17,25},{25,17},{2,10},{10... | collective-permute-start | bytes 786440 | tf_op jit(solution)/shard_map/ppermute | solution.py:408
  4.0 8.7 %collective-permute-start.1 = (bf16[272,2048]{1,0:T(8,128)(2,1)S(1)}, bf16[272,2048]{1,0:T(8,128)(2,1)S(1)}, u32[]{:S(2)}, u32[]{:S(2)}) collective-permute-start(bf16[272,2048]{1,0:T(8,128)(2,1)S(1)} %get-tuple-element.48), channel_id=1, source_target_pairs={{0,8},{8,0},{16,24},{24,16},{1,9},{9,1},{17,25},{25,17},{2,10},{10... | collective-permute-start | bytes 3342344 | tf_op jit(solution)/shard_map/ppermute | solution.py:409
  4.1 8.6 %collective-permute-start.2 = (bf16[2,64,512]{2,1,0:T(8,128)(2,1)S(1)}, bf16[2,64,512]{2,1,0:T(8,128)(2,1)S(1)}, u32[]{:S(2)}, u32[]{:S(2)}) collective-permute-start(bf16[2,64,512]{2,1,0:T(8,128)(2,1)S(1)} %get-tuple-element.50), channel_id=1, source_target_pairs={{0,2},{1,3},{2,0},{3,1},{4,6},{5,7},{6,4},{7,5},{8,10},{9,11},{10,... | collective-permute-start | bytes 393224 | tf_op jit(solution)/shard_map/ppermute | solution.py:386
  7.1 12.9 %collective-permute-start.5 = (bf16[2,64,512]{2,1,0:T(8,128)(2,1)S(1)}, bf16[2,64,512]{2,1,0:T(8,128)(2,1)S(1)}, u32[]{:S(2)}, u32[]{:S(2)}) collective-permute-start(bf16[2,64,512]{2,1,0:T(8,128)(2,1)S(1)} %get-tuple-element.53), channel_id=1, source_target_pairs={{0,4},{1,5},{2,6},{3,7},{4,0},{5,1},{6,2},{7,3},{8,12},{9,13},{10,... | collective-permute-start | bytes 393224 | tf_op jit(solution)/shard_map/ppermute | solution.py:386
  9.7 10.3 %collective-permute-start.6 = (bf16[2,64,512]{2,1,0:T(8,128)(2,1)S(1)}, bf16[2,64,512]{2,1,0:T(8,128)(2,1)S(1)}, u32[]{:S(2)}, u32[]{:S(2)}) collective-permute-start(bf16[2,64,512]{2,1,0:T(8,128)(2,1)S(1)} %get-tuple-element.54), channel_id=1, source_target_pairs={{0,6},{1,7},{2,4},{3,5},{4,2},{5,3},{6,0},{7,1},{8,14},{9,15},{10,... | collective-permute-start | bytes 393224 | tf_op jit(solution)/shard_map/ppermute | solution.py:386
  12.7 7.3 %collective-permute-start.3 = (bf16[128,512]{1,0:T(8,128)(2,1)S(1)}, bf16[128,512]{1,0:T(8,128)(2,1)S(1)}, u32[]{:S(2)}, u32[]{:S(2)}) collective-permute-start(bf16[128,512]{1,0:T(8,128)(2,1)S(1)} %get-tuple-element.51.rest_0_), channel_id=1, source_target_pairs={{0,16},{8,24},{16,0},{24,8},{1,17},{9,25},{17,1},{25,9},{2,18},{10... | collective-permute-start | bytes 393224 | tf_op jit(solution)/shard_map/ppermute | solution.py:392
  14.5 5.9 %collective-permute-start.4 = (bf16[128,512]{1,0:T(8,128)(2,1)S(1)}, bf16[128,512]{1,0:T(8,128)(2,1)S(1)}, u32[]{:S(2)}, u32[]{:S(2)}) collective-permute-start(bf16[128,512]{1,0:T(8,128)(2,1)S(1)} %get-tuple-element.52), channel_id=1, source_target_pairs={{0,17},{1,16},{2,19},{3,18},{4,21},{5,20},{6,23},{7,22},{8,25},{9,... | collective-permute-start | bytes 393224 | tf_op jit(solution)/shard_map/ppermute | solution.py:395
  15.9 8.0 %collective-permute-start.9 = (bf16[128,512]{1,0:T(8,128)(2,1)S(1)}, bf16[128,512]{1,0:T(8,128)(2,1)S(1)}, u32[]{:S(2)}, u32[]{:S(2)}) collective-permute-start(bf16[128,512]{1,0:T(8,128)(2,1)S(1)} %get-tuple-element.52), channel_id=1, source_target_pairs={{0,1},{1,0},{2,3},{3,2},{4,5},{5,4},{6,7},{7,6},{8,9},{9,8},{10,11... | collective-permute-start | bytes 393224 | tf_op jit(solution)/shard_map/ppermute | solution.py:389
  20.4 5.5 %collective-permute-start.10 = (bf16[128,512]{1,0:T(8,128)(2,1)S(1)}, bf16[128,512]{1,0:T(8,128)(2,1)S(1)}, u32[]{:S(2)}, u32[]{:S(2)}) collective-permute-start(bf16[128,512]{1,0:T(8,128)(2,1)S(1)} %get-tuple-element.56), channel_id=1, source_target_pairs={{0,1},{1,0},{2,3},{3,2},{4,5},{5,4},{6,7},{7,6},{8,9},{9,8},{10,11... | collective-permute-start | bytes 393224 | tf_op jit(solution)/shard_map/ppermute | solution.py:389
  22.0 9.1 %collective-permute-start.7 = (bf16[128,512]{1,0:T(8,128)(2,1)S(1)}, bf16[128,512]{1,0:T(8,128)(2,1)S(1)}, u32[]{:S(2)}, u32[]{:S(2)}) collective-permute-start(bf16[128,512]{1,0:T(8,128)(2,1)S(1)} %get-tuple-element.55.rest_2_), channel_id=1, source_target_pairs={{0,16},{8,24},{16,0},{24,8},{1,17},{9,25},{17,1},{25,9},{2,18},{10... | collective-permute-start | bytes 393224 | tf_op jit(solution)/shard_map/ppermute | solution.py:392
  23.1 9.0 %collective-permute-start.8 = (bf16[128,512]{1,0:T(8,128)(2,1)S(1)}, bf16[128,512]{1,0:T(8,128)(2,1)S(1)}, u32[]{:S(2)}, u32[]{:S(2)}) collective-permute-start(bf16[128,512]{1,0:T(8,128)(2,1)S(1)} %get-tuple-element.56), channel_id=1, source_target_pairs={{0,17},{1,16},{2,19},{3,18},{4,21},{5,20},{6,23},{7,22},{8,25},{9,... | collective-permute-start | bytes 393224 | tf_op jit(solution)/shard_map/ppermute | solution.py:395
  31.1 15.3 %collective-permute-start.11 = (bf16[256,512]{1,0:T(8,128)(2,1)S(1)}, bf16[256,512]{1,0:T(8,128)(2,1)S(1)}, u32[]{:S(2)}, u32[]{:S(2)}) collective-permute-start(bf16[256,512]{1,0:T(8,128)(2,1)S(1)} %shard_map.92), channel_id=1, source_target_pairs={{0,1},{1,0},{2,3},{3,2},{4,5},{5,4},{6,7},{7,6},{8,9},{9,8},{10,11... | collective-permute-start | bytes 786440 | tf_op jit(solution)/shard_map/ppermute | solution.py:389
  32.4 14.0 %collective-permute-start.12 = (bf16[128,512]{1,0:T(8,128)(2,1)S(1)}, bf16[128,512]{1,0:T(8,128)(2,1)S(1)}, u32[]{:S(2)}, u32[]{:S(2)}) collective-permute-start(bf16[128,512]{1,0:T(8,128)(2,1)S(1)} %get-tuple-element.63), channel_id=1, source_target_pairs={{0,16},{8,24},{16,0},{24,8},{1,17},{9,25},{17,1},{25,9},{2,18},{10... | collective-permute-start | bytes 393224 | tf_op jit(solution)/shard_map/ppermute | solution.py:392
  38.7 7.7 %collective-permute-start.13 = (bf16[128,512]{1,0:T(8,128)(2,1)S(1)}, bf16[128,512]{1,0:T(8,128)(2,1)S(1)}, u32[]{:S(2)}, u32[]{:S(2)}) collective-permute-start(bf16[128,512]{1,0:T(8,128)(2,1)S(1)} %get-tuple-element.64), channel_id=1, source_target_pairs={{0,17},{1,16},{2,19},{3,18},{4,21},{5,20},{6,23},{7,22},{8,25},{9,... | collective-permute-start | bytes 393224 | tf_op jit(solution)/shard_map/ppermute | solution.py:395
  39.9 11.0 %collective-permute-start.14 = (bf16[128,512]{1,0:T(8,128)(2,1)S(1)}, bf16[128,512]{1,0:T(8,128)(2,1)S(1)}, u32[]{:S(2)}, u32[]{:S(2)}) collective-permute-start(bf16[128,512]{1,0:T(8,128)(2,1)S(1)} %get-tuple-element.66), channel_id=1, source_target_pairs={{0,16},{8,24},{16,0},{24,8},{1,17},{9,25},{17,1},{25,9},{2,18},{10... | collective-permute-start | bytes 393224 | tf_op jit(solution)/shard_map/ppermute | solution.py:392
  40.0 10.9 %collective-permute-start.15 = (bf16[128,512]{1,0:T(8,128)(2,1)S(1)}, bf16[128,512]{1,0:T(8,128)(2,1)S(1)}, u32[]{:S(2)}, u32[]{:S(2)}) collective-permute-start(bf16[128,512]{1,0:T(8,128)(2,1)S(1)} %get-tuple-element.67), channel_id=1, source_target_pairs={{0,17},{1,16},{2,19},{3,18},{4,21},{5,20},{6,23},{7,22},{8,25},{9,... | collective-permute-start | bytes 393224 | tf_op jit(solution)/shard_map/ppermute | solution.py:395
  46.4 7.7 %collective-permute-start.20 = (bf16[2,64,512]{2,1,0:T(8,128)(2,1)S(1)}, bf16[2,64,512]{2,1,0:T(8,128)(2,1)S(1)}, u32[]{:S(2)}, u32[]{:S(2)}) collective-permute-start(bf16[2,64,512]{2,1,0:T(8,128)(2,1)S(1)} %get-tuple-element.73), channel_id=1, source_target_pairs={{0,6},{1,7},{2,4},{3,5},{4,2},{5,3},{6,0},{7,1},{8,14},{9,15},{10,... | collective-permute-start | bytes 393224 | tf_op jit(solution)/shard_map/ppermute | solution.py:386
  49.3 8.2 %collective-permute-start.19 = (bf16[2,64,512]{2,1,0:T(8,128)(2,1)S(1)}, bf16[2,64,512]{2,1,0:T(8,128)(2,1)S(1)}, u32[]{:S(2)}, u32[]{:S(2)}) collective-permute-start(bf16[2,64,512]{2,1,0:T(8,128)(2,1)S(1)} %get-tuple-element.65.refs_0_), channel_id=1, source_target_pairs={{0,4},{1,5},{2,6},{3,7},{4,0},{5,1},{6,2},{7,3},{8,12},{9,13},{10,... | collective-permute-start | bytes 393224 | tf_op jit(solution)/shard_map/ppermute | solution.py:386
  51.0 6.5 %collective-permute-start.18 = (bf16[2,64,512]{2,1,0:T(8,128)(2,1)S(1)}, bf16[2,64,512]{2,1,0:T(8,128)(2,1)S(1)}, u32[]{:S(2)}, u32[]{:S(2)}) collective-permute-start(bf16[2,64,512]{2,1,0:T(8,128)(2,1)S(1)} %get-tuple-element.72), channel_id=1, source_target_pairs={{0,2},{1,3},{2,0},{3,1},{4,6},{5,7},{6,4},{7,5},{8,10},{9,11},{10,... | collective-permute-start | bytes 393224 | tf_op jit(solution)/shard_map/ppermute | solution.py:386
  51.2 6.4 %collective-permute-start.16 = (bf16[64,2048]{1,0:T(8,128)(2,1)S(1)}, bf16[64,2048]{1,0:T(8,128)(2,1)S(1)}, u32[]{:S(2)}, u32[]{:S(2)}) collective-permute-start(bf16[64,2048]{1,0:T(8,128)(2,1)S(1)} %get-tuple-element.69), channel_id=1, source_target_pairs={{0,8},{8,0},{16,24},{24,16},{1,9},{9,1},{17,25},{25,17},{2,10},{10... | collective-permute-start | bytes 786440 | tf_op jit(solution)/shard_map/ppermute | solution.py:441
  51.3 6.3 %collective-permute-start.17 = (bf16[64,2048]{1,0:T(8,128)(2,1)S(1)}, bf16[64,2048]{1,0:T(8,128)(2,1)S(1)}, u32[]{:S(2)}, u32[]{:S(2)}) collective-permute-start(bf16[64,2048]{1,0:T(8,128)(2,1)S(1)} %get-tuple-element.70), channel_id=1, source_target_pairs={{0,8},{8,0},{16,24},{24,16},{1,9},{9,1},{17,25},{25,17},{2,10},{10... | collective-permute-start | bytes 786440 | tf_op jit(solution)/shard_map/ppermute | solution.py:441
  57.6 1.6 %collective-permute-start.21 = (bf16[2,8,16,512]{3,2,1,0:T(8,128)(2,1)S(1)}, bf16[2,8,16,512]{3,2,1,0:T(8,128)(2,1)S(1)}, u32[]{:S(2)}, u32[]{:S(2)}) collective-permute-start(bf16[2,8,16,512]{3,2,1,0:T(8,128)(2,1)S(1)} %get-tuple-element.77), channel_id=1, source_target_pairs={{0,8},{8,0},{16,24},{24,16},{1,9},{9,1},{17,25},{25,17},{2,10},{10... | collective-permute-start | bytes 786440 | tf_op jit(solution)/shard_map/ppermute | solution.py:512

commit v2 on v1

--- a/solution.py
+++ b/solution.py
@@ -21,7 +21,6 @@
 HALF_QCOLS = HALF_KCOLS * RATIO
 WIDE = RATIO * HD
 SAMP_ROWS = 16
-TILE = 256
 DQ_PARTS = 2
 SCALE = HD ** (-0.5)
 LOG2E = 1.4426950408889634
@@ -244,84 +243,85 @@
     if with_prev:
         prev, rest = rest[:2], rest[2:]
     rest = rest[n_through:]
-    dqs, grads, (ds_all, ph_all) = rest[:2], rest[2 : 2 + n_grads], rest[-2:]
+    dqs, grads = rest[:2], rest[2 : 2 + n_grads]
     sample = where()[0] ^ role
     tokens = g_a.shape[0]
     block_rows = SLOT_ROWS // n_blocks
     row_a = q_a[tokens : tokens + 1, :tokens].astype(F32)
     row_b = got[2 * tokens : 2 * tokens + 1, :tokens].astype(F32)
     wanted = sample.astype(F32)
-    has = jnp.where(row_a == wanted, 1.0, jnp.where(row_b == wanted, 1.0, 0.0))
-    present = jnp.max(has) > 0.5
-
-    @pl.when(present)
-    def _():
-        mine = jnp.concatenate([row_a] * RATIO + [row_b] * RATIO, axis=1) == wanted
-        for h in range(HALF_KV):
-            first_q = h * WIDE
-            first_k = h * HD
-            ds_ref, ph_ref = ds_all.at[h % 2], ph_all.at[h % 2]
-
-            def stacked(ref_a, first_b):
-                parts = [
-                    ref[first : first + tokens, first_q + r * HD : first_q + (r + 1) * HD]
-                    for ref, first in ((ref_a, 0), (got, first_b))
-                    for r in range(RATIO)
-                ]
+    rows = (row_a, row_b)
+    present = [jnp.max(jnp.where(row == wanted, 1.0, 0.0)) > 0.5 for row in rows]
+    sources = ((q_a, 0, g_a, 0), (got, 0, got, tokens))
+
+    def one_pass(which):
+        mine = jnp.concatenate([rows[t] for t in which for _ in range(RATIO)], axis=1) == wanted
+
+        def head(h, carry):
+            def stacked(part):
+                parts = []
+                for t in which:
+                    ref, first = sources[t][part : part + 2]
+                    wide = ref[first : first + tokens, at_cols(h * WIDE, WIDE, WIDE)]
+                    parts += [wide[:, r * HD : (r + 1) * HD] for r in range(RATIO)]
                 return jnp.concatenate(parts, axis=0)
 
             def rows_of(first):
                 parts = []
                 for kv in kvs:
                     for at in range(first, kv.shape[0], 2 * block_rows):
-                        parts.append(kv[at : at + block_rows, first_k : first_k + HD])
+                        parts.append(kv[at : at + block_rows, at_cols(h * HD, HD, HD)])
                 return jnp.concatenate(parts, axis=0)
 
-            q = stacked(q_a, 0)
-            g = stacked(g_a, tokens)
+            q = stacked(0)
+            g = stacked(2)
             k = rows_of(0)
             v = rows_of(block_rows)
-            for first in range(0, q.shape[0], TILE):
-                many = slice(first, first + TILE)
-                s = lax.dot_general(k, q[many], NT, preferred_element_type=F32)
-                gp = lax.dot_general(v, g[many], NT, preferred_element_type=F32)
-                for at in range(0, TILE, HD):
-                    one = slice(at, at + HD)
-                    here = slice(first + at, first + at + HD)
-                    part = s[:, one] + bias[role]
-                    top = jnp.max(part, axis=0, keepdims=True)
-                    e = jnp.exp2((part - top) * (SCALE * LOG2E))
-                    total = jnp.sum(e, axis=0, keepdims=True)
-                    p = e * jnp.where(mine[:, here], 1.0 / total, 0.0)
-                    row_dot = jnp.sum(p * gp[:, one], axis=0, keepdims=True)
-                    ds_ref[:, here] = (p * (gp[:, one] - row_dot)).astype(BF16)
-                    ph_ref[:, here] = p.astype(BF16)
-            ds = ds_ref[...]
-            dv = jnp.dot(ph_ref[...], g, preferred_element_type=F32)
+            s = lax.dot_general(k, q, NT, preferred_element_type=F32)
+            s = s + jnp.concatenate([bias[role]] * (s.shape[1] // HD), axis=1)
+            top = jnp.max(s, axis=0, keepdims=True)
+            e = jnp.exp2((s - top) * (SCALE * LOG2E))
+            total = jnp.sum(e, axis=0, keepdims=True)
+            p = e * jnp.where(mine, 1.0 / total, 0.0)
+            gp = lax.dot_general(v, g, NT, preferred_element_type=F32)
+            row_dot = jnp.sum(p * gp, axis=0, keepdims=True)
+            ds = (p * (gp - row_dot)).astype(BF16)
+            dv = jnp.dot(p.astype(BF16), g, preferred_element_type=F32)
             dk = jnp.dot(ds, q, preferred_element_type=F32) * SCALE
             dq = lax.dot_general(ds, k, TN, preferred_element_type=F32) * SCALE
-            for t, dq_ref in enumerate(dqs):
-                for r in range(RATIO):
-                    at = (t * RATIO + r) * tokens
-                    cols = slice(first_q + r * HD, first_q + (r + 1) * HD)
-                    part = dq[at : at + tokens]
-                    if with_prev:
-                        part = part + prev[t][:, cols].astype(F32)
-                    dq_ref[:, cols] = part.astype(dq_ref.dtype)
-            cols = slice(first_k, first_k + HD)
+            for i, t in enumerate(which):
+                cols = at_cols(h * WIDE, WIDE, WIDE)
+                at = i * RATIO * tokens
+                part = jnp.concatenate(
+                    [dq[at + r * tokens : at + (r + 1) * tokens] for r in range(RATIO)], axis=1
+                )
+                if with_prev:
+                    part = part + prev[t][:, cols].astype(F32)
+                dqs[t][:, cols] = part.astype(dqs[t].dtype)
+            cols = at_cols(h * HD, HD, HD)
             for b in range(n_blocks):
-                rows = slice(b * block_rows, (b + 1) * block_rows)
+                block = slice(b * block_rows, (b + 1) * block_rows)
                 dx, at = block_place(b, len(grads))
                 out, first = grads[dx], at * 2 * block_rows
-                out[first : first + block_rows, cols] = dk[rows].astype(out.dtype)
-                out[first + block_rows : first + 2 * block_rows, cols] = dv[rows].astype(out.dtype)
-
-    @pl.when(jnp.logical_not(present))
-    def _():
-        for out in grads:
-            out[...] = jnp.zeros_like(out)
-        for t, dq_ref in enumerate(dqs):
-            dq_ref[...] = prev[t][...] if with_prev else jnp.zeros_like(dq_ref)
+                out[first : first + block_rows, cols] = dk[block].astype(out.dtype)
+                out[first + block_rows : first + 2 * block_rows, cols] = dv[block].astype(out.dtype)
+            return carry
+
+        lax.fori_loop(0, HALF_KV, head, 0)
+
+    for which in ((0, 1), (0,), (1,), ()):
+        wants = [present[t] if t in which else jnp.logical_not(present[t]) for t in range(2)]
+
+        @pl.when(wants[0] & wants[1])
+        def _():
+            if which:
+                one_pass(which)
+            else:
+                for out in grads:
+                    out[...] = jnp.zeros_like(out)
+            for t in range(2):
+                if t not in which:
+                    dqs[t][...] = prev[t][...] if with_prev else jnp.zeros_like(dqs[t])
 
 
 def sample_pass(where, role, n_blocks, bias, text, kvs, prev, grads, through=()):
@@ -333,7 +333,6 @@
             pass_kernel, role, n_blocks, len(kvs), prev is not None, len(through), len(grads), where
         ),
         [dq, dq, *grads] + [(a.shape, a.dtype) for a in through],
-        scratch=[pltpu.VMEM((2, SLOT_ROWS, CORES * RATIO * tokens), BF16)] * 2,
         flops=10 * tokens * WIDE * SLOT_ROWS * CORES * HALF_KV,
         moved=16 * 2**20,
         aliases={len(args) + i: 2 + len(grads) + i for i in range(len(through))},

time: 60.2 us -> 58.5 us (0.972); the launches traced: 60 us -> 59.1 us
  transfers between devices with their start and end apart: 22 -> 22, of which waited for: 8 -> 8; matrix products, arithmetic and copies ran while one was open for 0% -> 0% of each run, Pallas kernels for 14% -> 13%
where the time goes in v2:
time: 58.5 us; the launch traced here: 59.1 us
  starting transfers between devices  28.8 us (49%)
  waiting for transfers between devices  19.7 us (34%)
  Pallas kernels  9.86 us (17%)
  between operations  0.79 us (1%)
    ppermute x6, waiting for transfers between devices, along_z(): lax.ppermute(part, 'enc', [(i, i ^ 2 * dz) for i in range(n_enc)])  12.5 us
    ppermute x6, starting transfers between devices, along_z(): lax.ppermute(part, 'enc', [(i, i ^ 2 * dz) for i in range(n_enc)])  10.5 us
    ppermute x4, starting transfers between devices, along_y(): return lax.ppermute(part, 'ctx', swap_y)  8.89 us
    pallas_call x11, Pallas kernels, call(): return local_call(body, [IN_VMEM] * len(args), spec, **more)(*args)  5.3 us
    ppermute x4, starting transfers between devices, along_xy(): return lax.ppermute(part, ('ctx', 'enc'), swap_xy)  5.09 us
    ppermute x4, waiting for transfers between devices, along_y(): return lax.ppermute(part, 'ctx', swap_y)  4.42 us
    ppermute x3, starting transfers between devices, along_x(): return lax.ppermute(part, 'enc', swap_x)  2.97 us
    ppermute x3, waiting for transfers between devices, along_x(): return lax.ppermute(part, 'enc', swap_x)  1.93 us
  transfers between devices with their start and end apart: 22, of which 8 were waited for; matrix products, arithmetic and copies ran while one was open for 0% of the time, Pallas kernels for 13%

profile of v2, /device:TPU:0, one launch (start us, length us, event | category | flops | bytes accessed | tf_op | source)
XLA Modules:
  0.0 59.1 jit_solution(3045686706949666416)
XLA Ops:
  0.6 1.1 %shard_map.86 = (bf16[2,8,16,512]{3,2,1,0:T(8,128)(2,1)S(1)}, bf16[2,8,16,512]{3,2,1,0:T(8,128)(2,1)S(1)}) custom-call(bf16[8,16,1024]{2,1,0:T(8,128)(2,1)} %k_ref.1, bf16[8,16,1024]{2,1,0:T(8,128)(2,1)} %v_ref.1), custom_call_target="tpu_custom_call" | custom-call | bytes 524288 | tf_op jit(solution)/shard_map/pallas_call | solution.py:396
  1.8 0.5 collective-permute-start
  2.3 1.6 %shard_map.85 = (bf16[272,2048]{1,0:T(8,128)(2,1)S(1)}, bf16[144,2048]{1,0:T(8,128)(2,1)S(1)}, bf16[128,2048]{1,0:T(8,128)(2,1)S(1)}, f32[2,256,128]{2,1,0:T(8,128)S(1)}) custom-call(bf16[1,128,4096]{2,1,0:T(8,128)(2,1)} %q_ref.1, bf16[1,128,4096]{2,1,0:T(8,128)(2,1)} %g_ref.1, s32[1,128]{1,0:T(1,128)} %samp_hbm.1, s32[1,2]{1,0:T(1,128)} %tiles_hbm.1), custom_call_target="tpu_custom_call" | custom-call | bytes 4194304 | tf_op jit(solution)/shard_map/pallas_call | solution.py:357
  3.9 0.0 collective-permute-done.got
  3.9 0.1 shard_map.87
  4.0 0.1 collective-permute-start.1
  4.1 3.0 %collective-permute-start.2 = (bf16[2,64,512]{2,1,0:T(8,128)(2,1)S(1)}, bf16[2,64,512]{2,1,0:T(8,128)(2,1)S(1)}, u32[]{:S(2)}, u32[]{:S(2)}) collective-permute-start(bf16[2,64,512]{2,1,0:T(8,128)(2,1)S(1)} %get-tuple-element.50), channel_id=1, source_target_pairs={{0,2},{1,3},{2,0},{3,1},{4,6},{5,7},{6,4},{7,5},{8,10},{9,11},{10,... | collective-permute-start | bytes 393224 | tf_op jit(solution)/shard_map/ppermute | solution.py:385
  7.1 2.6 %collective-permute-start.5 = (bf16[2,64,512]{2,1,0:T(8,128)(2,1)S(1)}, bf16[2,64,512]{2,1,0:T(8,128)(2,1)S(1)}, u32[]{:S(2)}, u32[]{:S(2)}) collective-permute-start(bf16[2,64,512]{2,1,0:T(8,128)(2,1)S(1)} %get-tuple-element.53), channel_id=1, source_target_pairs={{0,4},{1,5},{2,6},{3,7},{4,0},{5,1},{6,2},{7,3},{8,12},{9,13},{10,... | collective-permute-start | bytes 393224 | tf_op jit(solution)/shard_map/ppermute | solution.py:385
  9.7 0.0 collective-permute-start.6
  9.7 3.0 %collective-permute-done.2.refs_1_ = bf16[2,64,512]{2,1,0:T(8,128)(2,1)S(1)} collective-permute-done((bf16[2,64,512]{2,1,0:T(8,128)(2,1)S(1)}, bf16[2,64,512]{2,1,0:T(8,128)(2,1)S(1)}, u32[]{:S(2)}, u32[]{:S(2)}) %collective-permute-start.2) | collective-permute-done | bytes 131104 | tf_op jit(solution)/shard_map/ppermute | solution.py:385
  12.7 0.0 collective-permute-done.1.refs_2_.got
  12.7 1.8 %collective-permute-start.3 = (bf16[128,512]{1,0:T(8,128)(2,1)S(1)}, bf16[128,512]{1,0:T(8,128)(2,1)S(1)}, u32[]{:S(2)}, u32[]{:S(2)}) collective-permute-start(bf16[128,512]{1,0:T(8,128)(2,1)S(1)} %get-tuple-element.51.rest_0_), channel_id=1, source_target_pairs={{0,16},{8,24},{16,0},{24,8},{1,17},{9,25},{17,1},{25,9},{2,18},{10... | collective-permute-start | bytes 393224 | tf_op jit(solution)/shard_map/ppermute | solution.py:391
  14.5 1.4 %collective-permute-start.4 = (bf16[128,512]{1,0:T(8,128)(2,1)S(1)}, bf16[128,512]{1,0:T(8,128)(2,1)S(1)}, u32[]{:S(2)}, u32[]{:S(2)}) collective-permute-start(bf16[128,512]{1,0:T(8,128)(2,1)S(1)} %get-tuple-element.52), channel_id=1, source_target_pairs={{0,17},{1,16},{2,19},{3,18},{4,21},{5,20},{6,23},{7,22},{8,25},{9,... | collective-permute-start | bytes 393224 | tf_op jit(solution)/shard_map/ppermute | solution.py:394
  15.9 0.3 collective-permute-start.9
  16.3 3.8 %collective-permute-done.5.refs_0_ = bf16[2,64,512]{2,1,0:T(8,128)(2,1)S(1)} collective-permute-done((bf16[2,64,512]{2,1,0:T(8,128)(2,1)S(1)}, bf16[2,64,512]{2,1,0:T(8,128)(2,1)S(1)}, u32[]{:S(2)}, u32[]{:S(2)}) %collective-permute-start.5) | collective-permute-done | bytes 131104 | tf_op jit(solution)/shard_map/ppermute | solution.py:385
  20.0 0.0 collective-permute-done.6.refs_1_
  20.0 0.0 collective-permute-done.3.refs_3_.rest_0_
  20.0 0.3 collective-permute-done.4.refs_4_.rest_1_
  20.4 1.6 %collective-permute-start.10 = (bf16[128,512]{1,0:T(8,128)(2,1)S(1)}, bf16[128,512]{1,0:T(8,128)(2,1)S(1)}, u32[]{:S(2)}, u32[]{:S(2)}) collective-permute-start(bf16[128,512]{1,0:T(8,128)(2,1)S(1)} %get-tuple-element.56), channel_id=1, source_target_pairs={{0,1},{1,0},{2,3},{3,2},{4,5},{5,4},{6,7},{7,6},{8,9},{9,8},{10,11... | collective-permute-start | bytes 393224 | tf_op jit(solution)/shard_map/ppermute | solution.py:388
  22.0 1.2 %collective-permute-start.7 = (bf16[128,512]{1,0:T(8,128)(2,1)S(1)}, bf16[128,512]{1,0:T(8,128)(2,1)S(1)}, u32[]{:S(2)}, u32[]{:S(2)}) collective-permute-start(bf16[128,512]{1,0:T(8,128)(2,1)S(1)} %get-tuple-element.55.rest_2_), channel_id=1, source_target_pairs={{0,16},{8,24},{16,0},{24,8},{1,17},{9,25},{17,1},{25,9},{2,18},{10... | collective-permute-start | bytes 393224 | tf_op jit(solution)/shard_map/ppermute | solution.py:391
  23.1 0.8 %collective-permute-start.8 = (bf16[128,512]{1,0:T(8,128)(2,1)S(1)}, bf16[128,512]{1,0:T(8,128)(2,1)S(1)}, u32[]{:S(2)}, u32[]{:S(2)}) collective-permute-start(bf16[128,512]{1,0:T(8,128)(2,1)S(1)} %get-tuple-element.56), channel_id=1, source_target_pairs={{0,17},{1,16},{2,19},{3,18},{4,21},{5,20},{6,23},{7,22},{8,25},{9,... | collective-permute-start | bytes 393224 | tf_op jit(solution)/shard_map/ppermute | solution.py:394
  24.0 0.0 collective-permute-done.9.rest_1_
  24.0 1.9 %collective-permute-done.10.rest_3_ = bf16[128,512]{1,0:T(8,128)(2,1)S(1)} collective-permute-done((bf16[128,512]{1,0:T(8,128)(2,1)S(1)}, bf16[128,512]{1,0:T(8,128)(2,1)S(1)}, u32[]{:S(2)}, u32[]{:S(2)}) %collective-permute-start.10) | collective-permute-done | bytes 131104 | tf_op jit(solution)/shard_map/ppermute | solution.py:388
  25.9 4.8 %shard_map.90 = (bf16[128,2048]{1,0:T(8,128)(2,1)S(1)}, bf16[128,2048]{1,0:T(8,128)(2,1)S(1)}, f32[256,512]{1,0:T(8,128)S(1)}, bf16[256,512]{1,0:T(8,128)(2,1)S(1)}) custom-call(f32[2,256,128]{2,1,0:T(8,128)S(1)} %get-tuple-element.42.bias, bf16[144,2048]{1,0:T(8,128)(2,1)S(1)} %get-tuple-element.43.q_a, bf16[128,2048]{1,0:T(8,128)(2,1)S(1)} %get-tuple-element.44.g_a, ...), custom_call_target="tpu_custom_call" | custom-call | flops 1342177280 | bytes 16777216 | tf_op jit(solution)/shard_map/pallas_call | solution.py:55
  30.6 0.0 collective-permute-done.7.rest_2_.refs_1_
  30.7 1.1 %collective-permute-start.11 = (bf16[256,512]{1,0:T(8,128)(2,1)S(1)}, bf16[256,512]{1,0:T(8,128)(2,1)S(1)}, u32[]{:S(2)}, u32[]{:S(2)}) collective-permute-start(bf16[256,512]{1,0:T(8,128)(2,1)S(1)} %shard_map.92), channel_id=1, source_target_pairs={{0,1},{1,0},{2,3},{3,2},{4,5},{5,4},{6,7},{7,6},{8,9},{9,8},{10,11... | collective-permute-start | bytes 786440 | tf_op jit(solution)/shard_map/ppermute | solution.py:388
  31.8 0.2 shard_map.91
  32.0 5.7 %collective-permute-start.12 = (bf16[128,512]{1,0:T(8,128)(2,1)S(1)}, bf16[128,512]{1,0:T(8,128)(2,1)S(1)}, u32[]{:S(2)}, u32[]{:S(2)}) collective-permute-start(bf16[128,512]{1,0:T(8,128)(2,1)S(1)} %get-tuple-element.63), channel_id=1, source_target_pairs={{0,16},{8,24},{16,0},{24,8},{1,17},{9,25},{17,1},{25,9},{2,18},{10... | collective-permute-start | bytes 393224 | tf_op jit(solution)/shard_map/ppermute | solution.py:391
  37.8 0.0 collective-permute-start.13
  37.8 0.2 collective-permute-start.14
  37.9 2.8 %collective-permute-start.15 = (bf16[128,512]{1,0:T(8,128)(2,1)S(1)}, bf16[128,512]{1,0:T(8,128)(2,1)S(1)}, u32[]{:S(2)}, u32[]{:S(2)}) collective-permute-start(bf16[128,512]{1,0:T(8,128)(2,1)S(1)} %get-tuple-element.67), channel_id=1, source_target_pairs={{0,17},{1,16},{2,19},{3,18},{4,21},{5,20},{6,23},{7,22},{8,25},{9,... | collective-permute-start | bytes 393224 | tf_op jit(solution)/shard_map/ppermute | solution.py:394
  40.8 4.4 %collective-permute-done.12.back_y = bf16[128,512]{1,0:T(8,128)(2,1)S(1)} collective-permute-done((bf16[128,512]{1,0:T(8,128)(2,1)S(1)}, bf16[128,512]{1,0:T(8,128)(2,1)S(1)}, u32[]{:S(2)}, u32[]{:S(2)}) %collective-permute-start.12) | collective-permute-done | bytes 131104 | tf_op jit(solution)/shard_map/ppermute | solution.py:391
  45.2 0.1 shard_map.93
  45.2 4.2 %collective-permute-start.20 = (bf16[2,64,512]{2,1,0:T(8,128)(2,1)S(1)}, bf16[2,64,512]{2,1,0:T(8,128)(2,1)S(1)}, u32[]{:S(2)}, u32[]{:S(2)}) collective-permute-start(bf16[2,64,512]{2,1,0:T(8,128)(2,1)S(1)} %get-tuple-element.73), channel_id=1, source_target_pairs={{0,6},{1,7},{2,4},{3,5},{4,2},{5,3},{6,0},{7,1},{8,14},{9,15},{10,... | collective-permute-start | bytes 393224 | tf_op jit(solution)/shard_map/ppermute | solution.py:385
  49.5 0.6 %collective-permute-start.19 = (bf16[2,64,512]{2,1,0:T(8,128)(2,1)S(1)}, bf16[2,64,512]{2,1,0:T(8,128)(2,1)S(1)}, u32[]{:S(2)}, u32[]{:S(2)}) collective-permute-start(bf16[2,64,512]{2,1,0:T(8,128)(2,1)S(1)} %get-tuple-element.65.refs_0_), channel_id=1, source_target_pairs={{0,4},{1,5},{2,6},{3,7},{4,0},{5,1},{6,2},{7,3},{8,12},{9,13},{10,... | collective-permute-start | bytes 393224 | tf_op jit(solution)/shard_map/ppermute | solution.py:385
  50.1 0.1 shard_map.94
  50.1 0.1 collective-permute-start.18
  50.3 0.1 collective-permute-start.16
  50.3 0.5 collective-permute-start.17
  50.8 1.6 %collective-permute-done.20.refs_1_ = bf16[2,64,512]{2,1,0:T(8,128)(2,1)S(1)} collective-permute-done((bf16[2,64,512]{2,1,0:T(8,128)(2,1)S(1)}, bf16[2,64,512]{2,1,0:T(8,128)(2,1)S(1)}, u32[]{:S(2)}, u32[]{:S(2)}) %collective-permute-start.20) | collective-permute-done | bytes 131104 | tf_op jit(solution)/shard_map/ppermute | solution.py:385
  52.5 4.1 %collective-permute-done.19.refs_0_ = bf16[2,64,512]{2,1,0:T(8,128)(2,1)S(1)} collective-permute-done((bf16[2,64,512]{2,1,0:T(8,128)(2,1)S(1)}, bf16[2,64,512]{2,1,0:T(8,128)(2,1)S(1)}, u32[]{:S(2)}, u32[]{:S(2)}) %collective-permute-start.19) | collective-permute-done | bytes 131104 | tf_op jit(solution)/shard_map/ppermute | solution.py:385
  56.6 0.0 collective-permute-done.18.refs_1_
  56.6 0.1 shard_map.98
  56.7 0.1 collective-permute-start.21
  56.8 0.0 collective-permute-done.16.refs_0_
  56.8 1.0 %shard_map.96 = (bf16[1,128,4096]{2,1,0:T(8,128)(2,1)}, f32[8,128]{1,0:T(8,128)S(1)}) custom-call(bf16[128,2048]{1,0:T(8,128)(2,1)S(1)} %get-tuple-element.59.mine, bf16[64,2048]{1,0:T(8,128)(2,1)S(1)} %collective-permute-done.16.refs_0_, bf16[64,2048]{1,0:T(8,128)(2,1)S(1)} %collective-permute-done.17.refs_1_), custom_call_target="tpu_custom_call" | custom-call | bytes 524288 | tf_op jit(solution)/shard_map/pallas_call | solution.py:491
  57.8 0.5 collective-permute-done.21.got
  58.3 0.8 %shard_map.99 = (bf16[8,16,1024]{2,1,0:T(8,128)(2,1)}, bf16[8,16,1024]{2,1,0:T(8,128)(2,1)}) custom-call(bf16[2,8,16,512]{3,2,1,0:T(8,128)(2,1)S(1)} %get-tuple-element.76.mine, bf16[2,8,16,512]{3,2,1,0:T(8,128)(2,1)S(1)} %collective-permute-done.21.got, f32[8,128]{1,0:T(8,128)S(1)} %get-tuple-element.78._), custom_call_target="tpu_custom_call" | custom-call | bytes 524288 | tf_op jit(solution)/shard_map/pallas_call | solution.py:506
  (11 shorter events, 0.1 us)
Async XLA Ops:
  1.8 2.1 %collective-permute-start = (bf16[2,8,16,512]{3,2,1,0:T(8,128)(2,1)S(1)}, bf16[2,8,16,512]{3,2,1,0:T(8,128)(2,1)S(1)}, u32[]{:S(2)}, u32[]{:S(2)}) collective-permute-start(bf16[2,8,16,512]{3,2,1,0:T(8,128)(2,1)S(1)} %get-tuple-element.46), channel_id=1, source_target_pairs={{0,8},{8,0},{16,24},{24,16},{1,9},{9,1},{17,25},{25,17},{2,10},{10... | collective-permute-start | bytes 786440 | tf_op jit(solution)/shard_map/ppermute | solution.py:407
  4.0 8.7 %collective-permute-start.1 = (bf16[272,2048]{1,0:T(8,128)(2,1)S(1)}, bf16[272,2048]{1,0:T(8,128)(2,1)S(1)}, u32[]{:S(2)}, u32[]{:S(2)}) collective-permute-start(bf16[272,2048]{1,0:T(8,128)(2,1)S(1)} %get-tuple-element.48), channel_id=1, source_target_pairs={{0,8},{8,0},{16,24},{24,16},{1,9},{9,1},{17,25},{25,17},{2,10},{10... | collective-permute-start | bytes 3342344 | tf_op jit(solution)/shard_map/ppermute | solution.py:408
  4.1 8.6 %collective-permute-start.2 = (bf16[2,64,512]{2,1,0:T(8,128)(2,1)S(1)}, bf16[2,64,512]{2,1,0:T(8,128)(2,1)S(1)}, u32[]{:S(2)}, u32[]{:S(2)}) collective-permute-start(bf16[2,64,512]{2,1,0:T(8,128)(2,1)S(1)} %get-tuple-element.50), channel_id=1, source_target_pairs={{0,2},{1,3},{2,0},{3,1},{4,6},{5,7},{6,4},{7,5},{8,10},{9,11},{10,... | collective-permute-start | bytes 393224 | tf_op jit(solution)/shard_map/ppermute | solution.py:385
  7.1 12.9 %collective-permute-start.5 = (bf16[2,64,512]{2,1,0:T(8,128)(2,1)S(1)}, bf16[2,64,512]{2,1,0:T(8,128)(2,1)S(1)}, u32[]{:S(2)}, u32[]{:S(2)}) collective-permute-start(bf16[2,64,512]{2,1,0:T(8,128)(2,1)S(1)} %get-tuple-element.53), channel_id=1, source_target_pairs={{0,4},{1,5},{2,6},{3,7},{4,0},{5,1},{6,2},{7,3},{8,12},{9,13},{10,... | collective-permute-start | bytes 393224 | tf_op jit(solution)/shard_map/ppermute | solution.py:385
  9.7 10.3 %collective-permute-start.6 = (bf16[2,64,512]{2,1,0:T(8,128)(2,1)S(1)}, bf16[2,64,512]{2,1,0:T(8,128)(2,1)S(1)}, u32[]{:S(2)}, u32[]{:S(2)}) collective-permute-start(bf16[2,64,512]{2,1,0:T(8,128)(2,1)S(1)} %get-tuple-element.54), channel_id=1, source_target_pairs={{0,6},{1,7},{2,4},{3,5},{4,2},{5,3},{6,0},{7,1},{8,14},{9,15},{10,... | collective-permute-start | bytes 393224 | tf_op jit(solution)/shard_map/ppermute | solution.py:385
  12.7 7.3 %collective-permute-start.3 = (bf16[128,512]{1,0:T(8,128)(2,1)S(1)}, bf16[128,512]{1,0:T(8,128)(2,1)S(1)}, u32[]{:S(2)}, u32[]{:S(2)}) collective-permute-start(bf16[128,512]{1,0:T(8,128)(2,1)S(1)} %get-tuple-element.51.rest_0_), channel_id=1, source_target_pairs={{0,16},{8,24},{16,0},{24,8},{1,17},{9,25},{17,1},{25,9},{2,18},{10... | collective-permute-start | bytes 393224 | tf_op jit(solution)/shard_map/ppermute | solution.py:391
  14.5 5.9 %collective-permute-start.4 = (bf16[128,512]{1,0:T(8,128)(2,1)S(1)}, bf16[128,512]{1,0:T(8,128)(2,1)S(1)}, u32[]{:S(2)}, u32[]{:S(2)}) collective-permute-start(bf16[128,512]{1,0:T(8,128)(2,1)S(1)} %get-tuple-element.52), channel_id=1, source_target_pairs={{0,17},{1,16},{2,19},{3,18},{4,21},{5,20},{6,23},{7,22},{8,25},{9,... | collective-permute-start | bytes 393224 | tf_op jit(solution)/shard_map/ppermute | solution.py:394
  15.9 8.0 %collective-permute-start.9 = (bf16[128,512]{1,0:T(8,128)(2,1)S(1)}, bf16[128,512]{1,0:T(8,128)(2,1)S(1)}, u32[]{:S(2)}, u32[]{:S(2)}) collective-permute-start(bf16[128,512]{1,0:T(8,128)(2,1)S(1)} %get-tuple-element.52), channel_id=1, source_target_pairs={{0,1},{1,0},{2,3},{3,2},{4,5},{5,4},{6,7},{7,6},{8,9},{9,8},{10,11... | collective-permute-start | bytes 393224 | tf_op jit(solution)/shard_map/ppermute | solution.py:388
  20.4 5.5 %collective-permute-start.10 = (bf16[128,512]{1,0:T(8,128)(2,1)S(1)}, bf16[128,512]{1,0:T(8,128)(2,1)S(1)}, u32[]{:S(2)}, u32[]{:S(2)}) collective-permute-start(bf16[128,512]{1,0:T(8,128)(2,1)S(1)} %get-tuple-element.56), channel_id=1, source_target_pairs={{0,1},{1,0},{2,3},{3,2},{4,5},{5,4},{6,7},{7,6},{8,9},{9,8},{10,11... | collective-permute-start | bytes 393224 | tf_op jit(solution)/shard_map/ppermute | solution.py:388
  22.0 8.7 %collective-permute-start.7 = (bf16[128,512]{1,0:T(8,128)(2,1)S(1)}, bf16[128,512]{1,0:T(8,128)(2,1)S(1)}, u32[]{:S(2)}, u32[]{:S(2)}) collective-permute-start(bf16[128,512]{1,0:T(8,128)(2,1)S(1)} %get-tuple-element.55.rest_2_), channel_id=1, source_target_pairs={{0,16},{8,24},{16,0},{24,8},{1,17},{9,25},{17,1},{25,9},{2,18},{10... | collective-permute-start | bytes 393224 | tf_op jit(solution)/shard_map/ppermute | solution.py:391
  23.1 8.6 %collective-permute-start.8 = (bf16[128,512]{1,0:T(8,128)(2,1)S(1)}, bf16[128,512]{1,0:T(8,128)(2,1)S(1)}, u32[]{:S(2)}, u32[]{:S(2)}) collective-permute-start(bf16[128,512]{1,0:T(8,128)(2,1)S(1)} %get-tuple-element.56), channel_id=1, source_target_pairs={{0,17},{1,16},{2,19},{3,18},{4,21},{5,20},{6,23},{7,22},{8,25},{9,... | collective-permute-start | bytes 393224 | tf_op jit(solution)/shard_map/ppermute | solution.py:394
  30.7 14.5 %collective-permute-start.11 = (bf16[256,512]{1,0:T(8,128)(2,1)S(1)}, bf16[256,512]{1,0:T(8,128)(2,1)S(1)}, u32[]{:S(2)}, u32[]{:S(2)}) collective-permute-start(bf16[256,512]{1,0:T(8,128)(2,1)S(1)} %shard_map.92), channel_id=1, source_target_pairs={{0,1},{1,0},{2,3},{3,2},{4,5},{5,4},{6,7},{7,6},{8,9},{9,8},{10,11... | collective-permute-start | bytes 786440 | tf_op jit(solution)/shard_map/ppermute | solution.py:388
  32.0 13.2 %collective-permute-start.12 = (bf16[128,512]{1,0:T(8,128)(2,1)S(1)}, bf16[128,512]{1,0:T(8,128)(2,1)S(1)}, u32[]{:S(2)}, u32[]{:S(2)}) collective-permute-start(bf16[128,512]{1,0:T(8,128)(2,1)S(1)} %get-tuple-element.63), channel_id=1, source_target_pairs={{0,16},{8,24},{16,0},{24,8},{1,17},{9,25},{17,1},{25,9},{2,18},{10... | collective-permute-start | bytes 393224 | tf_op jit(solution)/shard_map/ppermute | solution.py:391
  37.8 7.4 %collective-permute-start.13 = (bf16[128,512]{1,0:T(8,128)(2,1)S(1)}, bf16[128,512]{1,0:T(8,128)(2,1)S(1)}, u32[]{:S(2)}, u32[]{:S(2)}) collective-permute-start(bf16[128,512]{1,0:T(8,128)(2,1)S(1)} %get-tuple-element.64), channel_id=1, source_target_pairs={{0,17},{1,16},{2,19},{3,18},{4,21},{5,20},{6,23},{7,22},{8,25},{9,... | collective-permute-start | bytes 393224 | tf_op jit(solution)/shard_map/ppermute | solution.py:394
  37.8 12.3 %collective-permute-start.14 = (bf16[128,512]{1,0:T(8,128)(2,1)S(1)}, bf16[128,512]{1,0:T(8,128)(2,1)S(1)}, u32[]{:S(2)}, u32[]{:S(2)}) collective-permute-start(bf16[128,512]{1,0:T(8,128)(2,1)S(1)} %get-tuple-element.66), channel_id=1, source_target_pairs={{0,16},{8,24},{16,0},{24,8},{1,17},{9,25},{17,1},{25,9},{2,18},{10... | collective-permute-start | bytes 393224 | tf_op jit(solution)/shard_map/ppermute | solution.py:391
  37.9 12.2 %collective-permute-start.15 = (bf16[128,512]{1,0:T(8,128)(2,1)S(1)}, bf16[128,512]{1,0:T(8,128)(2,1)S(1)}, u32[]{:S(2)}, u32[]{:S(2)}) collective-permute-start(bf16[128,512]{1,0:T(8,128)(2,1)S(1)} %get-tuple-element.67), channel_id=1, source_target_pairs={{0,17},{1,16},{2,19},{3,18},{4,21},{5,20},{6,23},{7,22},{8,25},{9,... | collective-permute-start | bytes 393224 | tf_op jit(solution)/shard_map/ppermute | solution.py:394
  45.2 7.2 %collective-permute-start.20 = (bf16[2,64,512]{2,1,0:T(8,128)(2,1)S(1)}, bf16[2,64,512]{2,1,0:T(8,128)(2,1)S(1)}, u32[]{:S(2)}, u32[]{:S(2)}) collective-permute-start(bf16[2,64,512]{2,1,0:T(8,128)(2,1)S(1)} %get-tuple-element.73), channel_id=1, source_target_pairs={{0,6},{1,7},{2,4},{3,5},{4,2},{5,3},{6,0},{7,1},{8,14},{9,15},{10,... | collective-permute-start | bytes 393224 | tf_op jit(solution)/shard_map/ppermute | solution.py:385
  49.5 7.2 %collective-permute-start.19 = (bf16[2,64,512]{2,1,0:T(8,128)(2,1)S(1)}, bf16[2,64,512]{2,1,0:T(8,128)(2,1)S(1)}, u32[]{:S(2)}, u32[]{:S(2)}) collective-permute-start(bf16[2,64,512]{2,1,0:T(8,128)(2,1)S(1)} %get-tuple-element.65.refs_0_), channel_id=1, source_target_pairs={{0,4},{1,5},{2,6},{3,7},{4,0},{5,1},{6,2},{7,3},{8,12},{9,13},{10,... | collective-permute-start | bytes 393224 | tf_op jit(solution)/shard_map/ppermute | solution.py:385
  50.1 6.5 %collective-permute-start.18 = (bf16[2,64,512]{2,1,0:T(8,128)(2,1)S(1)}, bf16[2,64,512]{2,1,0:T(8,128)(2,1)S(1)}, u32[]{:S(2)}, u32[]{:S(2)}) collective-permute-start(bf16[2,64,512]{2,1,0:T(8,128)(2,1)S(1)} %get-tuple-element.72), channel_id=1, source_target_pairs={{0,2},{1,3},{2,0},{3,1},{4,6},{5,7},{6,4},{7,5},{8,10},{9,11},{10,... | collective-permute-start | bytes 393224 | tf_op jit(solution)/shard_map/ppermute | solution.py:385
  50.3 6.5 %collective-permute-start.16 = (bf16[64,2048]{1,0:T(8,128)(2,1)S(1)}, bf16[64,2048]{1,0:T(8,128)(2,1)S(1)}, u32[]{:S(2)}, u32[]{:S(2)}) collective-permute-start(bf16[64,2048]{1,0:T(8,128)(2,1)S(1)} %get-tuple-element.69), channel_id=1, source_target_pairs={{0,8},{8,0},{16,24},{24,16},{1,9},{9,1},{17,25},{25,17},{2,10},{10... | collective-permute-start | bytes 786440 | tf_op jit(solution)/shard_map/ppermute | solution.py:440
  50.3 6.5 %collective-permute-start.17 = (bf16[64,2048]{1,0:T(8,128)(2,1)S(1)}, bf16[64,2048]{1,0:T(8,128)(2,1)S(1)}, u32[]{:S(2)}, u32[]{:S(2)}) collective-permute-start(bf16[64,2048]{1,0:T(8,128)(2,1)S(1)} %get-tuple-element.70), channel_id=1, source_target_pairs={{0,8},{8,0},{16,24},{24,16},{1,9},{9,1},{17,25},{25,17},{2,10},{10... | collective-permute-start | bytes 786440 | tf_op jit(solution)/shard_map/ppermute | solution.py:440
  56.7 1.6 %collective-permute-start.21 = (bf16[2,8,16,512]{3,2,1,0:T(8,128)(2,1)S(1)}, bf16[2,8,16,512]{3,2,1,0:T(8,128)(2,1)S(1)}, u32[]{:S(2)}, u32[]{:S(2)}) collective-permute-start(bf16[2,8,16,512]{3,2,1,0:T(8,128)(2,1)S(1)} %get-tuple-element.77), channel_id=1, source_target_pairs={{0,8},{8,0},{16,24},{24,16},{1,9},{9,1},{17,25},{25,17},{2,10},{10... | collective-permute-start | bytes 786440 | tf_op jit(solution)/shard_map/ppermute | solution.py:511
